TPU v7x, 256 devices: a whole 4x4x8 slice. The times are simulated.
256 devices in a mesh: uv: 32 (over y_hi, z, core), freq: 8 (over y_lo, x).
Axes of the slice: x: 4, y: 4 (y_hi: 2, y_lo: 2; y = y_hi * 2 + y_lo), z: 8, core: 2. Of those that a mesh axis runs over, the one named last changes fastest.
Arguments:
- visibility: float32 [8, 1024, 8, 128], P('freq', 'uv'), may hold values from -6 to 6
- uv_offset: float32 [8, 1024, 2, 128], P('freq', 'uv'), may hold values from -12 to 12
- w_offset: float32 [8, 1024, 128], P('freq', 'uv'), may hold values from -40 to 40
- taper: float32 [32, 32], replicated, may hold values from 0.2 to 1
- row_count: int32 [8, 1024], P('freq', 'uv'), may hold values from 1 to 128, as said below
- block_owner: int32 [8, 1024, 1], P('freq', 'uv'), may hold values from 0 to 31; in each aligned block of 32 rows (0 to 31, 32 to 63, ..., all dimensions but the last counted through in order) at most 2 rows name the same one
- block_slot: int32 [8, 1024], P('freq', 'uv'), may hold values from 0 to 15
- subgrid_offset: int32 [512, 2], P('uv'), may hold values from 0 to 96
Outputs:
- grid: float32 [4096, 8, 128], P(('uv', 'freq'))
Inputs may be any that keep to these rules, and one draw needn't show every extreme that they name: `block_owner`: among the 32 blocks of one device at most 2 name the same owner, a bound that some block reaches of them. `row_count`: some block has all 128 rows live.
All inputs are finite; a program needn't handle non-finite values.
Results may differ from a plain program's by a relative error of at most 0.0003.
Values sent between devices are 32-bit elements; how exact they have to be, the bound alone decides.
A program may use at most 64 MiB of HBM per device.

v0:
```python
import functools
import math

import jax
import jax.numpy as jnp
from jax import lax
from jax.experimental import pallas as pl
from jax.experimental.pallas import tpu as pltpu
from jax.sharding import PartitionSpec as P

SUB = 32
BLK = 128
TILE = 128
OWNERS = 32
GROUPS = 8
OWNED = 16
SLOTS = 64
ROWS = 24
MAX_GROUPS = 82

SIN_POLY = (
    6.283185302511503,
    -41.34170040531769,
    81.60513138580204,
    -76.7030153539128,
    42.02592698618416,
    -14.899846668691637,
    3.238137510515757,
)
COS_POLY = (
    0.9999999890590228,
    -19.739204499454026,
    64.93911745990036,
    -85.45013953095037,
    60.16763095136588,
    -25.96759924965491,
    6.528658162567069,
)


def sincos_turns(turns):
    f = turns - jnp.round(turns)
    z = f * f
    s = jnp.full_like(z, SIN_POLY[-1])
    c = jnp.full_like(z, COS_POLY[-1])
    for a, b in zip(SIN_POLY[-2::-1], COS_POLY[-2::-1]):
        s = s * z + a
        c = c * z + b
    return s * f, c


def split(x):
    hi = x.astype(jnp.bfloat16)
    lo = (x - hi.astype(jnp.float32)).astype(jnp.bfloat16)
    return hi, lo


def dot_nt(a, b):
    return lax.dot_general(a, b, (((1,), (1,)), ((), ())), preferred_element_type=jnp.float32)


def dot_nn(a, b):
    return lax.dot_general(a, b, (((1,), (0,)), ((), ())), preferred_element_type=jnp.float32)


def iota(shape, axis):
    return lax.broadcasted_iota(jnp.int32, shape, axis)


def exchange_kernel(
    inv, slot, count, vis, uvo, wo, got, info, send, recv, send_sem, recv_sem
):
    me = lax.axis_index("uv")
    barrier = pltpu.get_barrier_semaphore()

    def greet(k, carry):
        peer = lax.rem(me + k, OWNERS)
        pl.semaphore_signal(
            barrier, inc=1, device_id={"uv": peer}, device_id_type=pl.DeviceIdType.MESH
        )
        return carry

    lax.fori_loop(1, OWNERS, greet, 0)

    lane = iota((1, BLK), 1)

    def pack(o, carry):
        others = []
        for rank in range(2):
            entry = inv[2 * o + rank]
            used = entry > 0
            j = jnp.maximum(entry - 1, 0)
            send[pl.ds(o * ROWS + 8 * rank, 8), :] = jnp.where(used, vis[j], 0.0)
            live = jnp.where(used, count[j], 0)
            facts = jnp.where(lane == 0, slot[j], live).astype(jnp.float32)
            others += [uvo[j], wo[pl.ds(j, 1), :], facts]
        send[pl.ds(o * ROWS + 16, 8), :] = jnp.concatenate(others, 0)
        return carry

    lax.fori_loop(0, OWNERS, pack, 0)
    pl.semaphore_wait(barrier, OWNERS - 1)

    def copy_to(k):
        peer = lax.rem(me + k, OWNERS)
        return pltpu.make_async_remote_copy(
            src_ref=send.at[pl.ds(pl.multiple_of(peer * ROWS, 8), ROWS)],
            dst_ref=recv.at[pl.ds(pl.multiple_of(me * ROWS, 8), ROWS)],
            send_sem=send_sem.at[k],
            recv_sem=recv_sem.at[k],
            device_id={"uv": peer},
            device_id_type=pl.DeviceIdType.MESH,
        )

    def start(k, carry):
        copy_to(k).start()
        return carry

    lax.fori_loop(1, OWNERS, start, 0)
    own = pl.ds(pl.multiple_of(me * ROWS, 8), ROWS)
    recv[own, :] = send[own, :]

    def finish(k, carry):
        source = lax.rem(me + OWNERS - k, OWNERS)
        pltpu.make_async_remote_copy(
            src_ref=send.at[pl.ds(pl.multiple_of(source * ROWS, 8), ROWS)],
            dst_ref=recv.at[pl.ds(pl.multiple_of(source * ROWS, 8), ROWS)],
            send_sem=send_sem.at[k],
            recv_sem=recv_sem.at[k],
            device_id={"uv": source},
            device_id_type=pl.DeviceIdType.MESH,
        ).wait_recv()
        return carry

    lax.fori_loop(1, OWNERS, finish, 0)
    got[...] = recv[...]
    info[0:OWNERS, :] = recv[pl.ds(19, OWNERS, stride=ROWS), :].astype(jnp.int32)
    info[OWNERS:, :] = recv[pl.ds(23, OWNERS, stride=ROWS), :].astype(jnp.int32)

    def drain(k, carry):
        copy_to(k).wait_send()
        return carry

    lax.fori_loop(1, OWNERS, drain, 0)


def exchange(inv, slot, count, vis, uvo, wo):
    smem = pl.BlockSpec(memory_space=pltpu.SMEM)
    vmem = pl.BlockSpec(memory_space=pltpu.VMEM)
    return pl.pallas_call(
        exchange_kernel,
        out_shape=(
            jax.ShapeDtypeStruct((OWNERS * ROWS, BLK), jnp.float32),
            jax.ShapeDtypeStruct((SLOTS, BLK), jnp.int32),
        ),
        in_specs=[smem] * 3 + [vmem] * 3,
        out_specs=(vmem, vmem),
        scratch_shapes=[
            pltpu.VMEM((OWNERS * ROWS, BLK), jnp.float32),
            pltpu.VMEM((OWNERS * ROWS, BLK), jnp.float32),
            pltpu.SemaphoreType.DMA((OWNERS,)),
            pltpu.SemaphoreType.DMA((OWNERS,)),
        ],
        compiler_params=pltpu.CompilerParams(collective_id=0, has_side_effects=True),
        name="exchange",
    )(inv, slot, count, vis, uvo, wo)


N_PHASE = 216
ROW_B = 64
ROW_C = 192
ROW_M = 208
ROW_U = 216
ROW_V = 232
N_TRIG = 248


def grid_kernel(
    info,
    offset,
    taper,
    got,
    tile,
    total,
    base,
    slot_of,
    buf,
    ntab,
    sines,
    cosines,
    c_hi,
    c_lo,
    d_hi,
    d_lo,
    acc,
    acc_edge,
    spread,
):
    def clear_total(s, carry):
        total[s] = 0
        return carry

    lax.fori_loop(0, OWNED, clear_total, 0)

    def add_total(b, carry):
        s = info[b, 0]
        total[s] = total[s] + info[b, 1]
        return carry

    lax.fori_loop(0, SLOTS, add_total, 0)

    def place_slot(s, first):
        number = lax.div(total[s] + (BLK - 1), BLK)
        base[s] = first * BLK

        def name_group(i, carry):
            slot_of[first + i] = s
            return carry

        lax.fori_loop(0, number, name_group, 0)
        return first + number

    groups = lax.fori_loop(0, OWNED, place_slot, 0)

    def clear_group(g, carry):
        buf[g] = jnp.zeros((16, BLK), jnp.float32)
        return carry

    lax.fori_loop(0, groups + 2, clear_group, 0)
    lane8 = iota((8, BLK), 1)

    def compact(i, carry):
        others = got[pl.ds(i * ROWS + 16, 8), :]
        for rank in range(2):
            b = i + OWNERS * rank
            s = info[b, 0]
            n = info[b, 1]
            at = base[s]
            base[s] = at + n
            g = lax.div(at, BLK)
            shift = at - g * BLK
            vis = pltpu.roll(got[pl.ds(i * ROWS + 8 * rank, 8), :], shift, 1)
            rest = pltpu.roll(others if rank == 0 else pltpu.roll(others, 4, 0), shift, 1)
            here = (lane8 >= shift) & (lane8 < shift + n)
            after = lane8 < shift + n - BLK
            buf[g, 0:8, :] = jnp.where(here, vis, buf[g, 0:8, :])
            buf[g, 8:16, :] = jnp.where(here, rest, buf[g, 8:16, :])
            buf[g + 1, 0:8, :] = jnp.where(after, vis, buf[g + 1, 0:8, :])
            buf[g + 1, 8:16, :] = jnp.where(after, rest, buf[g + 1, 8:16, :])
        return carry

    lax.fori_loop(0, OWNERS, compact, 0)

    def n_of(a, b):
        l = b * (0.5 / SUB)
        m = a * (0.5 / SUB)
        return 1.0 - jnp.sqrt(1.0 - l * l - m * m)

    row = iota((8, BLK), 0).astype(jnp.float32)
    for a in range(8):
        ntab[a * 8 : a * 8 + 8, :] = n_of(float(a), row)
    for a in range(8, 17):
        for h in range(2):
            at = ROW_B + (a - 8) * 16 + 8 * h
            ntab[at : at + 8, :] = n_of(float(a), row + 8.0 * h)
    ntab[ROW_M : ROW_M + 8, :] = jnp.where(
        row < 2.0, 16 * 0.5 / SUB, n_of(16.0, jnp.full((8, BLK), 16.0, jnp.float32))
    )
    step0 = row * (0.5 / SUB)
    step1 = (row + 8.0) * (0.5 / SUB)

    for s in range(OWNED):
        acc[s] = jnp.zeros((2, BLK, 2 * BLK), jnp.float32)
        acc_edge[s] = jnp.zeros((16, BLK), jnp.float32)

    first_row = iota((8, BLK), 0) == 0
    halves = jnp.where(iota((8, BLK), 0) < 4, 1.0, -1.0)

    def one_group(g, carry):
        u = buf[g, 8:9, :]
        v = buf[g, 9:10, :]
        w = buf[g, 10:11, :]

        def keep(at, turns):
            s, c = sincos_turns(turns)
            sines[at : at + 8, :] = s
            cosines[at : at + 8, :] = c

        for at in range(0, ROW_M, 8):
            keep(at, w * ntab[at : at + 8, :])
        sub = iota((8, BLK), 0)
        keep(ROW_M, jnp.where(sub == 0, u, jnp.where(sub == 1, v, w)) * ntab[ROW_M : ROW_M + 8, :])
        keep(ROW_U, u * step0)
        keep(ROW_U + 8, u * step1)
        keep(ROW_V, v * step0)
        keep(ROW_V + 8, v * step1)

        cu0 = cosines[ROW_U : ROW_U + 8, :]
        cu1 = cosines[ROW_U + 8 : ROW_U + 16, :]
        su0 = sines[ROW_U : ROW_U + 8, :]
        su1 = sines[ROW_U + 8 : ROW_U + 16, :]
        cu2 = jnp.where(first_row, cosines[ROW_M : ROW_M + 1, :], cu0)
        su2 = jnp.where(first_row, sines[ROW_M : ROW_M + 1, :], su0)

        for a in range(17):
            if a < 8:
                p0 = slice(a * 8, a * 8 + 8)
                p1 = pl.ds(ROW_B + a, 8, stride=16)
                edge = slice(ROW_C + a, ROW_C + a + 1)
            elif a < 16:
                p0 = slice(ROW_B + (a - 8) * 16, ROW_B + (a - 8) * 16 + 8)
                p1 = slice(ROW_B + (a - 8) * 16 + 8, ROW_B + (a - 8) * 16 + 16)
                edge = slice(ROW_C + a, ROW_C + a + 1)
            else:
                p0 = slice(ROW_C, ROW_C + 8)
                p1 = slice(ROW_C + 8, ROW_C + 16)
                edge = slice(ROW_M + 2, ROW_M + 3)
            cw0, sw0 = cosines[p0, :], sines[p0, :]
            cw1, sw1 = cosines[p1, :], sines[p1, :]
            cw2 = jnp.where(first_row, cosines[edge, :], cw0)
            sw2 = jnp.where(first_row, sines[edge, :], sw0)
            cc, ss, sc, cs = cw1 * cu1, sw1 * su1, sw1 * cu1, cw1 * su1
            cos_rows = [cw0 * cu0 - sw0 * su0, cc - ss, cw2 * cu2 + sw2 * su2, cc + ss]
            sin_rows = [sw0 * cu0 + cw0 * su0, sc + cs, sw2 * cu2 - cw2 * su2, sc - cs]
            for part, rows in enumerate((cos_rows, sin_rows)):
                hi, lo = split(jnp.concatenate(rows, 0))
                c_hi[a * 32 : a * 32 + 32, part * BLK : part * BLK + BLK] = hi
                c_lo[a * 32 : a * 32 + 32, part * BLK : part * BLK + BLK] = lo

        vis = buf[g, 0:8, :]
        swapped = pltpu.roll(vis, 4, 0) * halves
        for a in range(17):
            if a < 16:
                cv = cosines[ROW_V + a : ROW_V + a + 1, :]
                sv = sines[ROW_V + a : ROW_V + a + 1, :]
                left = jnp.concatenate([vis * cv, swapped * sv], 0)
                right = jnp.concatenate([swapped * cv, vis * -sv], 0)
            else:
                cv = cosines[ROW_M + 1 : ROW_M + 2, :]
                sv = sines[ROW_M + 1 : ROW_M + 2, :]
                nothing = jnp.zeros((8, BLK), jnp.float32)
                left = jnp.concatenate([vis * cv - swapped * sv, nothing], 0)
                right = jnp.concatenate([swapped * cv + vis * sv, nothing], 0)
            for part, rows in enumerate((left, right)):
                hi, lo = split(rows)
                d_hi[a * 16 : a * 16 + 16, part * BLK : part * BLK + BLK] = hi
                d_lo[a * 16 : a * 16 + 16, part * BLK : part * BLK + BLK] = lo

        s = slot_of[g]
        for t in range(2):
            dh = d_hi[t * 128 : t * 128 + 128, :]
            dl = d_lo[t * 128 : t * 128 + 128, :]
            ch = c_hi[t * 256 : t * 256 + 256, :]
            cl = c_lo[t * 256 : t * 256 + 256, :]
            acc[s, t] += dot_nt(dh, ch) + dot_nt(dl, ch) + dot_nt(dh, cl)
        dh, dl = d_hi[256:272, :], d_lo[256:272, :]
        ch, cl = c_hi[512:544, :], c_lo[512:544, :]
        acc_edge[s, :, 0:32] += dot_nt(dh, ch) + dot_nt(dl, ch) + dot_nt(dh, cl)
        return carry

    lax.fori_loop(0, groups, one_group, 0)

    col = iota((SUB, 2 * BLK), 1) % SUB
    col = jnp.where(col < 16, col + 16, jnp.where(col == 16, 0, 32 - col))
    pick = (iota((SUB, 2 * BLK), 0) == col).astype(jnp.float32)
    wide = lax.dot_general(
        taper[...], pick, (((1,), (0,)), ((), ())), precision=lax.Precision.HIGHEST,
        preferred_element_type=jnp.float32,
    ) * (1.0 / math.sqrt(BLK))
    place = lax.div(iota((1, 2 * BLK), 1), SUB)

    xr = iota((SUB, BLK), 0)
    xr = jnp.where(xr < 16, xr + 16, jnp.where(xr == 16, 0, 32 - xr))
    kx = iota((SUB, BLK), 1)
    sx, cx = sincos_turns((xr * kx % SUB).astype(jnp.float32) * (1.0 / SUB))
    table_re = jnp.where(kx < SUB, cx * (1.0 / SUB), 0.0)
    table_im = jnp.where(kx < SUB, sx * (-1.0 / SUB), 0.0)

    for s in range(OWNED):
        pieces = []
        for y in range(SUB):
            a = abs(y - 16)
            if a == 16:
                x = jnp.concatenate([acc_edge[s, 0:8, :], jnp.zeros((8, BLK), jnp.float32)], 1)
            else:
                even = acc[s, a // 8, (a % 8) * 16 : (a % 8) * 16 + 8, :]
                odd = acc[s, a // 8, (a % 8) * 16 + 8 : (a % 8) * 16 + 16, :]
                x = even + odd if y >= 16 else even - odd
            pieces.append(x * jnp.where(place == a % 8, wide[y : y + 1, :], 0.0))
        x_hi, x_lo = split(jnp.concatenate(pieces, 0))
        right = offset[s, 1]
        spun = jnp.concatenate(
            [pltpu.roll(table_re, right, 1), pltpu.roll(table_im, right, 1)], 1
        )
        t_hi, t_lo = split(spun)
        t_hi = jnp.concatenate([t_hi] * 8, 0)
        t_lo = jnp.concatenate([t_lo] * 8, 0)
        z = dot_nn(x_hi, t_hi) + dot_nn(x_lo, t_hi) + dot_nn(x_hi, t_lo)
        z_re = z[:, 0:BLK].reshape(SUB, 8, BLK)
        z_im = z[:, BLK:].reshape(SUB, 8, BLK)
        for y in range(SUB):
            spread[s * 256 + y * 8 : s * 256 + y * 8 + 8, :] = (
                z_re[y] - pltpu.roll(z_im[y], 4, 0) * halves
            )

    lane = iota((1, OWNED * SUB), 1)
    corner = jnp.zeros((1, OWNED * SUB), jnp.int32)
    for s in range(OWNED):
        corner = jnp.where(lax.div(lane, SUB) == s, offset[s, 0], corner)
    ky = iota((TILE, OWNED * SUB), 0) - corner
    yy = iota((TILE, OWNED * SUB), 1) % SUB
    sy, cy = sincos_turns(((ky * yy) & (SUB - 1)).astype(jnp.float32) * (1.0 / SUB))
    inside = (ky >= 0) & (ky < SUB)
    h = jnp.concatenate([jnp.where(inside, cy, 0.0), jnp.where(inside, -sy, 0.0)], 0)
    h_hi, h_lo = split(h)
    for p in range(4):
        both = jnp.concatenate(
            [
                spread[pl.ds(p, OWNED * SUB, stride=8), :],
                spread[pl.ds(p + 4, OWNED * SUB, stride=8), :],
            ],
            1,
        )
        b_hi, b_lo = split(both)
        o = dot_nn(h_hi, b_hi) + dot_nn(h_hi, b_lo) + dot_nn(h_lo, b_hi)
        tile[:, p, :] = o[0:TILE, 0:BLK] - o[TILE:, BLK:]
        tile[:, p + 4, :] = o[0:TILE, BLK:] + o[TILE:, 0:BLK]


def grid_tile(info, offset, taper, got):
    smem = pl.BlockSpec(memory_space=pltpu.SMEM)
    vmem = pl.BlockSpec(memory_space=pltpu.VMEM)
    f32, bf16 = jnp.float32, jnp.bfloat16
    return pl.pallas_call(
        grid_kernel,
        out_shape=jax.ShapeDtypeStruct((TILE, 8, TILE), f32),
        in_specs=[smem, smem, vmem, vmem],
        out_specs=vmem,
        scratch_shapes=[
            pltpu.SMEM((OWNED,), jnp.int32),
            pltpu.SMEM((OWNED,), jnp.int32),
            pltpu.SMEM((MAX_GROUPS,), jnp.int32),
            pltpu.VMEM((MAX_GROUPS, 16, BLK), f32),
            pltpu.VMEM((N_PHASE, BLK), f32),
            pltpu.VMEM((N_TRIG, BLK), f32),
            pltpu.VMEM((N_TRIG, BLK), f32),
            pltpu.VMEM((544, 2 * BLK), bf16),
            pltpu.VMEM((544, 2 * BLK), bf16),
            pltpu.VMEM((272, 2 * BLK), bf16),
            pltpu.VMEM((272, 2 * BLK), bf16),
            pltpu.VMEM((OWNED, 2, BLK, 2 * BLK), f32),
            pltpu.VMEM((OWNED, 16, BLK), f32),
            pltpu.VMEM((OWNED * SUB * 8, BLK), f32),
        ],
        compiler_params=pltpu.CompilerParams(vmem_limit_bytes=48 * 1024 * 1024),
        name="grid_tile",
    )(info, offset, taper, got)


def sum_kernel(tile, out, recv, send_sem, recv_sem):
    me = lax.axis_index("freq")
    barrier = pltpu.get_barrier_semaphore()
    for k in range(1, GROUPS):
        pl.semaphore_signal(
            barrier,
            inc=1,
            device_id={"freq": lax.rem(me + k, GROUPS)},
            device_id_type=pl.DeviceIdType.MESH,
        )
    pl.semaphore_wait(barrier, GROUPS - 1)
    strip = TILE // GROUPS
    copies = []
    for k in range(1, GROUPS):
        peer = lax.rem(me + k, GROUPS)
        copy = pltpu.make_async_remote_copy(
            src_ref=tile.at[pl.ds(peer * strip, strip)],
            dst_ref=recv.at[k],
            send_sem=send_sem.at[k],
            recv_sem=recv_sem.at[k],
            device_id={"freq": peer},
            device_id_type=pl.DeviceIdType.MESH,
        )
        copy.start()
        copies.append(copy)
    value = tile[pl.ds(me * strip, strip)]
    for k in range(1, GROUPS):
        copies[k - 1].wait_recv()
        value = value + recv[k]
    out[...] = value
    for copy in copies:
        copy.wait_send()


def sum_over_freq(tile):
    vmem = pl.BlockSpec(memory_space=pltpu.VMEM)
    strip = TILE // GROUPS
    return pl.pallas_call(
        sum_kernel,
        out_shape=jax.ShapeDtypeStruct((strip, 8, TILE), jnp.float32),
        in_specs=[vmem],
        out_specs=vmem,
        scratch_shapes=[
            pltpu.VMEM((GROUPS, strip, 8, TILE), jnp.float32),
            pltpu.SemaphoreType.DMA((GROUPS,)),
            pltpu.SemaphoreType.DMA((GROUPS,)),
        ],
        compiler_params=pltpu.CompilerParams(collective_id=1, has_side_effects=True),
        name="sum_over_freq",
    )(tile)


def shards(
    visibility, uv_offset, w_offset, taper, row_count, block_owner, block_slot, subgrid_offset
):
    owner = block_owner[0, :, 0]
    blocks = owner.shape[0]
    index = jnp.arange(blocks, dtype=jnp.int32)
    same = (owner[:, None] == owner[None, :]) & (index[None, :] < index[:, None])
    target = 2 * owner + jnp.sum(same.astype(jnp.int32), axis=1)
    inv = jnp.sum(
        jnp.where(
            target[None, :] == jnp.arange(SLOTS, dtype=jnp.int32)[:, None], index[None, :] + 1, 0
        ),
        axis=1,
    )
    got, info = exchange(
        inv, block_slot[0], row_count[0], visibility[0], uv_offset[0], w_offset[0]
    )
    return sum_over_freq(grid_tile(info, subgrid_offset, taper, got))


def solution(mesh):
    placed = (
        P("freq", "uv", None, None),
        P("freq", "uv", None, None),
        P("freq", "uv", None),
        P(),
        P("freq", "uv"),
        P("freq", "uv", None),
        P("freq", "uv"),
        P("uv", None),
    )
    return jax.shard_map(
        shards, mesh=mesh, in_specs=placed, out_specs=P(("uv", "freq"), None, None), check_vma=False
    )
```

profile of v0, /device:TPU:1, one launch (start us, length us, event | category | flops | bytes accessed | tf_op | source)
XLA Modules:
  0.0 76.1 jit_solution(8645927059656387050)
XLA Ops:
  0.0 0.0 copy-start.5
  0.0 0.7 copy-done.5
  0.7 0.2 convert_reduce_fusion
  0.8 0.0 copy-start.4
  0.9 0.6 select_reduce_fusion.inv
  1.5 0.1 copy-done.4
  1.5 0.1 copy.10.offset
  1.6 0.0 copy-start.3
  1.6 23.9 %exchange.1 = (f32[768,128]{1,0:T(8,128)}, s32[64,128]{1,0:T(8,128)}) custom-call(s32[64]{0:T(128)} %select_reduce_fusion.inv, s32[32]{0:T(128)} %bitcast.10, s32[32]{0:T(128)} %bitcast.11, f32[32,8,128]{2,1,0:T(8,128)} %bitcast.7, f32[32,2,128]{2,1,0:T(2,128)} %bitcast.8, f32[32,128]{1,0:T(8,128)} %bitcast.9), custom_call_target="tpu_custom_call" | custom-call | tf_op jit(solution)/shard_map/exchange/pallas_call | solution.py:149
  25.5 0.0 copy-done.3
  25.5 0.0 copy-start.1
  25.6 1.0 %copy-done.1 = f32[768,128]{1,0:T(8,128)S(1)} copy-done((f32[768,128]{1,0:T(8,128)S(1)}, f32[768,128]{1,0:T(8,128)}, u32[]{:S(2)}) %copy-start.1) | copy-done | bytes 393240
  26.5 0.0 copy-start.2
  26.5 0.8 copy-done.2
  27.3 33.9 %grid_tile.1.tile = f32[128,8,128]{2,1,0:T(8,128)S(1)} custom-call(s32[64,128]{1,0:T(8,128)S(1)} %copy-done.2, s32[16,2]{1,0:T(8,128)S(1)} %copy.10.offset, f32[32,32]{1,0:T(8,128)S(1)} %copy-done.3, f32[768,128]{1,0:T(8,128)S(1)} %copy-done.1), custom_call_target="tpu_custom_call" | custom-call | tf_op jit(solution)/shard_map/grid_tile/pallas_call | solution.py:433
  61.2 0.0 copy-start
  61.2 0.8 %copy-done = f32[128,8,128]{2,1,0:T(8,128)} copy-done((f32[128,8,128]{2,1,0:T(8,128)}, f32[128,8,128]{2,1,0:T(8,128)S(1)}, u32[]{:S(2)}) %copy-start) | copy-done | bytes 524312
  62.0 12.6 %sum_over_freq.1 = f32[16,8,128]{2,1,0:T(8,128)} custom-call(f32[128,8,128]{2,1,0:T(8,128)} %copy-done), custom_call_target="tpu_custom_call" | custom-call | tf_op jit(solution)/shard_map/sum_over_freq/pallas_call | solution.py:496
  74.7 1.5 %copy.12 = f32[16,8,128]{2,1,0:T(8,128)} copy(f32[16,8,128]{2,1,0:T(8,128)} %sum_over_freq.1) | data formatting | bytes 131072
  (1 shorter events, 0.0 us)
Async XLA Ops:
  0.0 0.7 copy-start.5
  0.8 0.7 copy-start.4
  1.6 23.9 %copy-start.3 = (f32[32,32]{1,0:T(8,128)S(1)}, f32[32,32]{1,0:T(8,128)}, u32[]{:S(2)}) copy-start(f32[32,32]{1,0:T(8,128)} %taper.1) | copy-start | bytes 12292
  25.5 1.0 %copy-start.1 = (f32[768,128]{1,0:T(8,128)S(1)}, f32[768,128]{1,0:T(8,128)}, u32[]{:S(2)}) copy-start(f32[768,128]{1,0:T(8,128)} %get-tuple-element.8.got) | copy-start | bytes 1179652
  26.5 0.8 copy-start.2
  61.2 0.8 %copy-start = (f32[128,8,128]{2,1,0:T(8,128)}, f32[128,8,128]{2,1,0:T(8,128)S(1)}, u32[]{:S(2)}) copy-start(f32[128,8,128]{2,1,0:T(8,128)S(1)} %grid_tile.1.tile) | copy-start | bytes 1572868
where the time goes:
time: 76.4 us; the launch traced here: 76.1 us
  Pallas kernels  70.5 us (92%)
  local copies, waits for them, and re-layouts  4.82 us (6%)
  other arithmetic  0.79 us (1%)
    pallas_call x1, Pallas kernels, grid_tile(): pl.pallas_call(grid_kernel, out_shape=jax.ShapeDtypeStruct((TILE, 8, TILE...  33.9 us
    pallas_call x1, Pallas kernels, exchange(): pl.pallas_call(exchange_kernel, out_shape=(jax.ShapeDtypeStruct((OWNERS *...  23.9 us
    pallas_call x1, Pallas kernels, sum_over_freq(): pl.pallas_call(sum_kernel, out_shape=jax.ShapeDtypeStruct((strip, 8, TILE...  12.6 us
    unnamed x14, local copies, waits for them, and re-layouts  4.82 us

commit v1 on v0

v1 whole, which is shorter than its diff:
```python
import functools
import math

import jax
import jax.numpy as jnp
from jax import lax
from jax.experimental import pallas as pl
from jax.experimental.pallas import tpu as pltpu
from jax.sharding import PartitionSpec as P

SUB = 32
BLK = 128
TILE = 128
OWNERS = 32
GROUPS = 8
OWNED = 16
SLOTS = 64
ROWS = 24
MAX_GROUPS = 82

SIN_POLY = (
    4.442882919124345,
    -7.308245686509104,
    3.6063542184332804,
    -0.8461116503752865,
    0.10982451642699691,
)
COS_POLY = (
    1.4142135620618328,
    -6.97886410988463,
    5.7398815391730755,
    -1.8882749233647587,
    0.3322515355413188,
    -0.03450161282339655,
)


def horner(z, coefficients):
    value = z * coefficients[-1] + coefficients[-2]
    for c in coefficients[-3::-1]:
        value = value * z + c
    return value


def sincos_turns(turns):
    f = turns - jnp.round(turns)
    z = f * f
    s = horner(z, SIN_POLY) * f
    c = horner(z, COS_POLY)
    return s * c, 1.0 - s * s


def split(x):
    hi = x.astype(jnp.bfloat16)
    lo = (x - hi.astype(jnp.float32)).astype(jnp.bfloat16)
    return hi, lo


def dot_nt(a, b):
    return lax.dot_general(a, b, (((1,), (1,)), ((), ())), preferred_element_type=jnp.float32)


def dot_nn(a, b):
    return lax.dot_general(a, b, (((1,), (0,)), ((), ())), preferred_element_type=jnp.float32)


def iota(shape, axis):
    return lax.broadcasted_iota(jnp.int32, shape, axis)


def exchange_kernel(
    inv, slot, count, vis, uvo, wo, got, info, send, recv, send_sem, recv_sem
):
    me = lax.axis_index("uv")
    barrier = pltpu.get_barrier_semaphore()

    def greet(k, carry):
        peer = lax.rem(me + k, OWNERS)
        pl.semaphore_signal(
            barrier, inc=1, device_id={"uv": peer}, device_id_type=pl.DeviceIdType.MESH
        )
        return carry

    lax.fori_loop(1, OWNERS, greet, 0)

    lane = iota((1, BLK), 1)

    def pack(o, carry):
        others = []
        for rank in range(2):
            entry = inv[2 * o + rank]
            used = entry > 0
            j = jnp.maximum(entry - 1, 0)
            send[pl.ds(o * ROWS + 8 * rank, 8), :] = jnp.where(used, vis[j], 0.0)
            live = jnp.where(used, count[j], 0)
            facts = jnp.where(lane == 0, slot[j], live).astype(jnp.float32)
            others += [uvo[j], wo[pl.ds(j, 1), :], facts]
        send[pl.ds(o * ROWS + 16, 8), :] = jnp.concatenate(others, 0)
        return carry

    lax.fori_loop(0, OWNERS, pack, 0)
    pl.semaphore_wait(barrier, OWNERS - 1)

    def copy_to(k):
        peer = lax.rem(me + k, OWNERS)
        return pltpu.make_async_remote_copy(
            src_ref=send.at[pl.ds(pl.multiple_of(peer * ROWS, 8), ROWS)],
            dst_ref=recv.at[pl.ds(pl.multiple_of(me * ROWS, 8), ROWS)],
            send_sem=send_sem.at[k],
            recv_sem=recv_sem.at[k],
            device_id={"uv": peer},
            device_id_type=pl.DeviceIdType.MESH,
        )

    def start(k, carry):
        copy_to(k).start()
        return carry

    lax.fori_loop(1, OWNERS, start, 0)
    own = pl.ds(pl.multiple_of(me * ROWS, 8), ROWS)
    recv[own, :] = send[own, :]

    def finish(k, carry):
        source = lax.rem(me + OWNERS - k, OWNERS)
        pltpu.make_async_remote_copy(
            src_ref=send.at[pl.ds(pl.multiple_of(source * ROWS, 8), ROWS)],
            dst_ref=recv.at[pl.ds(pl.multiple_of(source * ROWS, 8), ROWS)],
            send_sem=send_sem.at[k],
            recv_sem=recv_sem.at[k],
            device_id={"uv": source},
            device_id_type=pl.DeviceIdType.MESH,
        ).wait_recv()
        return carry

    lax.fori_loop(1, OWNERS, finish, 0)
    got[...] = recv[...]
    info[0:OWNERS, :] = recv[pl.ds(19, OWNERS, stride=ROWS), :].astype(jnp.int32)
    info[OWNERS:, :] = recv[pl.ds(23, OWNERS, stride=ROWS), :].astype(jnp.int32)

    def drain(k, carry):
        copy_to(k).wait_send()
        return carry

    lax.fori_loop(1, OWNERS, drain, 0)


def exchange(inv, slot, count, vis, uvo, wo):
    smem = pl.BlockSpec(memory_space=pltpu.SMEM)
    vmem = pl.BlockSpec(memory_space=pltpu.VMEM)
    return pl.pallas_call(
        exchange_kernel,
        out_shape=(
            jax.ShapeDtypeStruct((OWNERS * ROWS, BLK), jnp.float32),
            jax.ShapeDtypeStruct((SLOTS, BLK), jnp.int32),
        ),
        in_specs=[smem] * 3 + [vmem] * 3,
        out_specs=(vmem, vmem),
        scratch_shapes=[
            pltpu.VMEM((OWNERS * ROWS, BLK), jnp.float32),
            pltpu.VMEM((OWNERS * ROWS, BLK), jnp.float32),
            pltpu.SemaphoreType.DMA((OWNERS,)),
            pltpu.SemaphoreType.DMA((OWNERS,)),
        ],
        compiler_params=pltpu.CompilerParams(collective_id=0, has_side_effects=True),
        name="exchange",
    )(inv, slot, count, vis, uvo, wo)


N_PHASE = 216
ROW_B = 64
ROW_C = 192
ROW_M = 208
ROW_U = 216
ROW_V = 232
N_TRIG = 248
TILE_A = (tuple(range(8)) + (16,), tuple(range(8, 16)))
C_ROWS = (0, 9 * 32, 17 * 32)


def phases(g, buf, ntab, sines, cosines, c_part, d_part):
    u = buf[g, 8:9, :]
    v = buf[g, 9:10, :]
    w = buf[g, 10:11, :]
    sub = iota((8, BLK), 0)
    row = sub.astype(jnp.float32)
    first_row = sub == 0
    halves = jnp.where(sub < 4, 1.0, -1.0)
    step0 = row * (0.5 / SUB)
    step1 = (row + 8.0) * (0.5 / SUB)

    def keep(at, turns):
        s, c = sincos_turns(turns)
        sines[at : at + 8, :] = s
        cosines[at : at + 8, :] = c

    keep(ROW_M, jnp.where(sub == 0, u, jnp.where(sub == 1, v, w)) * ntab[ROW_M : ROW_M + 8, :])
    keep(ROW_U, u * step0)
    keep(ROW_U + 8, u * step1)
    keep(ROW_V, v * step0)
    keep(ROW_V + 8, v * step1)
    for at in range(0, ROW_M, 8):
        keep(at, w * ntab[at : at + 8, :])

    vis = buf[g, 0:8, :]
    swapped = pltpu.roll(vis, 4, 0) * halves
    for t in range(2):
        cv = cosines[ROW_V + 8 * t : ROW_V + 8 * t + 8, :]
        sv = sines[ROW_V + 8 * t : ROW_V + 8 * t + 8, :]
        if t == 0:
            c16 = jnp.where(first_row, cosines[ROW_M + 1 : ROW_M + 2, :], 0.0)
            sv = jnp.where(first_row, -sines[ROW_M + 1 : ROW_M + 2, :], sv)
        for c in range(8):
            one = jnp.broadcast_to(vis[c : c + 1, :], (8, BLK))
            two = jnp.broadcast_to(swapped[c : c + 1, :], (8, BLK))
            at = t * 128 + c * 16
            left, right = two * sv, -(one * sv)
            if t == 0:
                left, right = left + one * c16, right + two * c16
            d_part[at : at + 8, 0:BLK] = one * cv
            d_part[at : at + 8, BLK:] = two * cv
            d_part[at + 8 : at + 16, 0:BLK] = left
            d_part[at + 8 : at + 16, BLK:] = right

    cu0 = cosines[ROW_U : ROW_U + 8, :]
    cu1 = cosines[ROW_U + 8 : ROW_U + 16, :]
    su0 = sines[ROW_U : ROW_U + 8, :]
    su1 = sines[ROW_U + 8 : ROW_U + 16, :]
    cu2 = jnp.where(first_row, cosines[ROW_M : ROW_M + 1, :], cu0)
    su2 = jnp.where(first_row, sines[ROW_M : ROW_M + 1, :], su0)
    for t in range(2):
        for i, a in enumerate(TILE_A[t]):
            if a < 8:
                p0 = slice(a * 8, a * 8 + 8)
                p1 = pl.ds(ROW_B + a, 8, stride=16)
                edge = slice(ROW_C + a, ROW_C + a + 1)
            elif a < 16:
                p0 = slice(ROW_B + (a - 8) * 16, ROW_B + (a - 8) * 16 + 8)
                p1 = slice(ROW_B + (a - 8) * 16 + 8, ROW_B + (a - 8) * 16 + 16)
                edge = slice(ROW_C + a, ROW_C + a + 1)
            else:
                p0 = slice(ROW_C, ROW_C + 8)
                p1 = slice(ROW_C + 8, ROW_C + 16)
                edge = slice(ROW_M + 2, ROW_M + 3)
            cw0, sw0 = cosines[p0, :], sines[p0, :]
            cw1, sw1 = cosines[p1, :], sines[p1, :]
            cw2 = jnp.where(first_row, cosines[edge, :], cw0)
            sw2 = jnp.where(first_row, sines[edge, :], sw0)
            cc, ss, sc, cs = cw1 * cu1, sw1 * su1, sw1 * cu1, cw1 * su1
            cos_rows = [cw0 * cu0 - sw0 * su0, cc - ss, cw2 * cu2 + sw2 * su2, cc + ss]
            sin_rows = [sw0 * cu0 + cw0 * su0, sc + cs, sw2 * cu2 - cw2 * su2, sc - cs]
            at = C_ROWS[t] + i * 32
            for part, rows in enumerate((cos_rows, sin_rows)):
                for k in range(4):
                    c_part[at + 8 * k : at + 8 * k + 8, part * BLK : part * BLK + BLK] = rows[k]


def add_images(s, c_part, d_part, acc):
    lane = iota((SUB, BLK), 1)
    for t in range(2):
        d_both = jnp.concatenate(split(d_part[t * 128 : t * 128 + 128, :]), 0)
        c_hi, c_lo = split(c_part[C_ROWS[t] : C_ROWS[t + 1], :])
        o_hi = dot_nt(c_hi, d_both)
        o_lo = dot_nt(c_lo, d_both)
        total = None
        for i, a in enumerate(TILE_A[t]):
            hi = o_hi[i * 32 : i * 32 + 32, :]
            lo = o_lo[i * 32 : i * 32 + 32, 0:BLK]
            value = hi[:, 0:BLK] + hi[:, BLK:] + lo
            if total is None:
                total = value
            elif a == 16:
                total = jnp.where((lane & 15) == 8, value, total)
            else:
                total = jnp.where((lane & 7) == i, value, total)
        acc[s, t] += total


def grid_kernel(
    info,
    offset,
    taper,
    got,
    tile,
    total,
    base,
    slot_of,
    buf,
    ntab,
    sines_0,
    cosines_0,
    c_0,
    d_0,
    sines_1,
    cosines_1,
    c_1,
    d_1,
    acc,
    spread,
):
    def clear_total(s, carry):
        total[s] = 0
        return carry

    lax.fori_loop(0, OWNED, clear_total, 0)

    def add_total(b, carry):
        s = info[b, 0]
        total[s] = total[s] + info[b, 1]
        return carry

    lax.fori_loop(0, SLOTS, add_total, 0)
    slot_of[0] = OWNED

    def place_slot(s, first):
        number = lax.div(total[s] + (BLK - 1), BLK)
        base[s] = first * BLK

        def name_group(i, carry):
            slot_of[first + i + 1] = s
            return carry

        lax.fori_loop(0, number, name_group, 0)
        return first + number

    groups = lax.fori_loop(0, OWNED, place_slot, 0)
    slot_of[groups + 1] = OWNED

    def clear_group(g, carry):
        buf[g] = jnp.zeros((16, BLK), jnp.float32)
        return carry

    lax.fori_loop(0, groups + 2, clear_group, 0)
    lane8 = iota((8, BLK), 1)

    def compact(k, carry):
        moved = []
        for i4 in range(4):
            i = k * 4 + i4
            others = got[pl.ds(i * ROWS + 16, 8), :]
            for rank in range(2):
                b = i + OWNERS * rank
                s = info[b, 0]
                n = info[b, 1]
                at = base[s]
                base[s] = at + n
                g = lax.shift_right_logical(at, 7)
                shift = at & (BLK - 1)
                vis = pltpu.roll(got[pl.ds(i * ROWS + 8 * rank, 8), :], shift, 1)
                rest = pltpu.roll(others if rank == 0 else pltpu.roll(others, 4, 0), shift, 1)
                here = (lane8 >= shift) & (lane8 < shift + n)
                after = lane8 < shift + n - BLK
                moved.append((g, vis, rest, here, after))
        for g, vis, rest, here, after in moved:
            buf[g, 0:8, :] = jnp.where(here, vis, buf[g, 0:8, :])
            buf[g, 8:16, :] = jnp.where(here, rest, buf[g, 8:16, :])
            buf[g + 1, 0:8, :] = jnp.where(after, vis, buf[g + 1, 0:8, :])
            buf[g + 1, 8:16, :] = jnp.where(after, rest, buf[g + 1, 8:16, :])
        return carry

    lax.fori_loop(0, OWNERS // 4, compact, 0)

    def n_of(a, b):
        l = b * (0.5 / SUB)
        m = a * (0.5 / SUB)
        return 1.0 - jnp.sqrt(1.0 - l * l - m * m)

    row = iota((8, BLK), 0).astype(jnp.float32)
    for a in range(8):
        ntab[a * 8 : a * 8 + 8, :] = n_of(float(a), row)
    for a in range(8, 17):
        for h in range(2):
            at = ROW_B + (a - 8) * 16 + 8 * h
            ntab[at : at + 8, :] = n_of(float(a), row + 8.0 * h)
    ntab[ROW_M : ROW_M + 8, :] = jnp.where(
        row < 2.0, 16 * 0.5 / SUB, n_of(16.0, jnp.full((8, BLK), 16.0, jnp.float32))
    )

    for s in range(OWNED):
        acc[s] = jnp.zeros((2, SUB, BLK), jnp.float32)

    def two_groups(i, carry):
        g = 2 * i
        phases(g, buf, ntab, sines_0, cosines_0, c_0, d_0)
        add_images(slot_of[g], c_1, d_1, acc)
        phases(g + 1, buf, ntab, sines_1, cosines_1, c_1, d_1)
        add_images(slot_of[g + 1], c_0, d_0, acc)
        return carry

    steps = lax.div(groups + 1, 2)
    lax.fori_loop(0, steps, two_groups, 0)
    add_images(slot_of[2 * steps], c_1, d_1, acc)

    def y_of(high, sign, low):
        i = high * 8 + low
        return jnp.where(sign == 0, 16 + i, jnp.where(i == 0, 0, 16 - i))

    def x_of(j):
        return jnp.where(j < 16, j + 16, jnp.where(j == 16, 0, 32 - j))

    def exact(a, b, dims):
        return lax.dot_general(
            a, b, (dims, ((), ())), precision=lax.Precision.HIGHEST,
            preferred_element_type=jnp.float32,
        )

    pick_x = (x_of(iota((SUB, SUB), 0)) == iota((SUB, SUB), 1)).astype(jnp.float32)
    place = iota((SUB, 2 * BLK), 1)
    pick_y = (
        y_of(lax.shift_right_logical(place, 7), lax.shift_right_logical(place, 3) & 1, place & 7)
        == iota((SUB, 2 * BLK), 0)
    ).astype(jnp.float32)
    weight = exact(exact(pick_x, taper[...], ((1,), (1,))), pick_y, ((1,), (0,))) * (
        1.0 / math.sqrt(BLK)
    )

    xr = x_of(iota((SUB, BLK), 0))
    kx = iota((SUB, BLK), 1)
    sx, cx = sincos_turns((xr * kx & (SUB - 1)).astype(jnp.float32) * (1.0 / SUB))
    table_re = jnp.where(kx < SUB, cx * (1.0 / SUB), 0.0)
    table_im = jnp.where(kx < SUB, sx * (-1.0 / SUB), 0.0)
    lane = iota((SUB, BLK), 1)
    even_lane = (lane & 8) == 0
    nothing = jnp.zeros((SUB, 2 * BLK), jnp.bfloat16)

    for q in range(OWNED // 4):
        rows = []
        for s in range(4 * q, 4 * q + 4):
            both = []
            for t in range(2):
                a = acc[s, t]
                y = jnp.where(even_lane, a + pltpu.roll(a, BLK - 8, 1), pltpu.roll(a, 8, 1) - a)
                if t == 0:
                    y = jnp.where((lane & 7) == 0, a, y)
                both.append(y)
            rows.append(jnp.concatenate(both, 1) * weight)
        image = jnp.transpose(jnp.concatenate(rows, 0))
        x_hi, x_lo = split(image)
        x_both = jnp.concatenate([x_hi, x_lo], 1)
        for j in range(4):
            s = 4 * q + j
            right = offset[s, 1]
            t_hi, t_lo = split(
                jnp.concatenate(
                    [pltpu.roll(table_re, right, 1), pltpu.roll(table_im, right, 1)], 1
                )
            )
            w_hi = jnp.concatenate([nothing] * j + [t_hi] + [nothing] * (3 - j), 0)
            w_lo = jnp.concatenate([nothing] * j + [t_lo] + [nothing] * (3 - j), 0)
            z = dot_nn(x_both, jnp.concatenate([w_hi, w_hi], 0)) + dot_nn(x_hi, w_lo)
            for t in range(2):
                for p in range(4):
                    re = z[t * 128 + p * 16 : t * 128 + p * 16 + 16, :]
                    im = z[t * 128 + p * 16 + 64 : t * 128 + p * 16 + 80, :]
                    at = s * SUB + t * 16
                    spread[p, at : at + 16, 0:BLK] = re[:, 0:BLK] - im[:, BLK:]
                    spread[p, at : at + 16, BLK:] = re[:, BLK:] + im[:, 0:BLK]

    lane = iota((1, OWNED * SUB), 1)
    corner = jnp.zeros((1, OWNED * SUB), jnp.int32)
    for s in range(OWNED):
        corner = jnp.where(lax.shift_right_logical(lane, 5) == s, offset[s, 0], corner)
    ky = iota((TILE, OWNED * SUB), 0) - corner
    yy = y_of(lax.shift_right_logical(lane, 4) & 1, lax.shift_right_logical(lane, 3) & 1, lane & 7)
    sy, cy = sincos_turns(((ky * yy) & (SUB - 1)).astype(jnp.float32) * (1.0 / SUB))
    inside = (ky >= 0) & (ky < SUB)
    h = jnp.concatenate([jnp.where(inside, cy, 0.0), jnp.where(inside, -sy, 0.0)], 0)
    h_hi, h_lo = split(h)
    for p in range(4):
        b_hi, b_lo = split(spread[p])
        o = dot_nn(h_hi, b_hi) + dot_nn(h_hi, b_lo) + dot_nn(h_lo, b_hi)
        tile[p] = o[0:TILE, 0:BLK] - o[TILE:, BLK:]
        tile[p + 4] = o[0:TILE, BLK:] + o[TILE:, 0:BLK]


def grid_tile(info, offset, taper, got):
    smem = pl.BlockSpec(memory_space=pltpu.SMEM)
    vmem = pl.BlockSpec(memory_space=pltpu.VMEM)
    f32 = jnp.float32
    factors = [
        pltpu.VMEM((N_TRIG, BLK), f32),
        pltpu.VMEM((N_TRIG, BLK), f32),
        pltpu.VMEM((C_ROWS[2], 2 * BLK), f32),
        pltpu.VMEM((256, 2 * BLK), f32),
    ]
    return pl.pallas_call(
        grid_kernel,
        out_shape=jax.ShapeDtypeStruct((8, TILE, TILE), f32),
        in_specs=[smem, smem, vmem, vmem],
        out_specs=vmem,
        scratch_shapes=[
            pltpu.SMEM((OWNED,), jnp.int32),
            pltpu.SMEM((OWNED,), jnp.int32),
            pltpu.SMEM((MAX_GROUPS + 2,), jnp.int32),
            pltpu.VMEM((MAX_GROUPS, 16, BLK), f32),
            pltpu.VMEM((N_PHASE, BLK), f32),
            *factors,
            *factors,
            pltpu.VMEM((OWNED + 1, 2, SUB, BLK), f32),
            pltpu.VMEM((4, OWNED * SUB, 2 * BLK), f32),
        ],
        compiler_params=pltpu.CompilerParams(vmem_limit_bytes=62 * 1024 * 1024),
        name="grid_tile",
    )(info, offset, taper, got)


def sum_kernel(tile, out, recv, send_sem, recv_sem):
    me = lax.axis_index("freq")
    barrier = pltpu.get_barrier_semaphore()
    for k in range(1, GROUPS):
        pl.semaphore_signal(
            barrier,
            inc=1,
            device_id={"freq": lax.rem(me + k, GROUPS)},
            device_id_type=pl.DeviceIdType.MESH,
        )
    pl.semaphore_wait(barrier, GROUPS - 1)
    strip = TILE // GROUPS
    copies = []
    for k in range(1, GROUPS):
        peer = lax.rem(me + k, GROUPS)
        copy = pltpu.make_async_remote_copy(
            src_ref=tile.at[:, pl.ds(pl.multiple_of(peer * strip, 8), strip)],
            dst_ref=recv.at[k],
            send_sem=send_sem.at[k],
            recv_sem=recv_sem.at[k],
            device_id={"freq": peer},
            device_id_type=pl.DeviceIdType.MESH,
        )
        copy.start()
        copies.append(copy)
    value = tile[:, pl.ds(pl.multiple_of(me * strip, 8), strip), :]
    for k in range(1, GROUPS):
        copies[k - 1].wait_recv()
        value = value + recv[k]
    for c in range(8):
        out[:, c, :] = value[c]
    for copy in copies:
        copy.wait_send()


def sum_over_freq(tile):
    vmem = pl.BlockSpec(memory_space=pltpu.VMEM)
    strip = TILE // GROUPS
    return pl.pallas_call(
        sum_kernel,
        out_shape=jax.ShapeDtypeStruct((strip, 8, TILE), jnp.float32),
        in_specs=[vmem],
        out_specs=vmem,
        scratch_shapes=[
            pltpu.VMEM((GROUPS, 8, strip, TILE), jnp.float32),
            pltpu.SemaphoreType.DMA((GROUPS,)),
            pltpu.SemaphoreType.DMA((GROUPS,)),
        ],
        compiler_params=pltpu.CompilerParams(collective_id=1, has_side_effects=True),
        name="sum_over_freq",
    )(tile)


def shards(
    visibility, uv_offset, w_offset, taper, row_count, block_owner, block_slot, subgrid_offset
):
    owner = block_owner[0, :, 0]
    blocks = owner.shape[0]
    index = jnp.arange(blocks, dtype=jnp.int32)
    same = (owner[:, None] == owner[None, :]) & (index[None, :] < index[:, None])
    target = 2 * owner + jnp.sum(same.astype(jnp.int32), axis=1)
    inv = jnp.sum(
        jnp.where(
            target[None, :] == jnp.arange(SLOTS, dtype=jnp.int32)[:, None], index[None, :] + 1, 0
        ),
        axis=1,
    )
    got, info = exchange(
        inv, block_slot[0], row_count[0], visibility[0], uv_offset[0], w_offset[0]
    )
    return sum_over_freq(grid_tile(info, subgrid_offset, taper, got))


def solution(mesh):
    placed = (
        P("freq", "uv", None, None),
        P("freq", "uv", None, None),
        P("freq", "uv", None),
        P(),
        P("freq", "uv"),
        P("freq", "uv", None),
        P("freq", "uv"),
        P("uv", None),
    )
    return jax.shard_map(
        shards, mesh=mesh, in_specs=placed, out_specs=P(("uv", "freq"), None, None), check_vma=False
    )
```

time: 76.4 us -> 60 us (0.79)
  the two profiles are of different devices: /device:TPU:1 before, /device:TPU:32 now
where the time goes in v1:
time: 60 us; the launch traced here: 59.7 us
  Pallas kernels  56 us (93%)
  local copies, waits for them, and re-layouts  2.81 us (5%)
  other arithmetic  0.87 us (1%)
    pallas_call x1, Pallas kernels, grid_tile(): pl.pallas_call(grid_kernel, out_shape=jax.ShapeDtypeStruct((8, TILE, TILE...  24.4 us
    pallas_call x1, Pallas kernels, exchange(): pl.pallas_call(exchange_kernel, out_shape=(jax.ShapeDtypeStruct((OWNERS *...  21.8 us
    pallas_call x1, Pallas kernels, sum_over_freq(): pl.pallas_call(sum_kernel, out_shape=jax.ShapeDtypeStruct((strip, 8, TILE...  9.74 us
    unnamed x6, local copies, waits for them, and re-layouts  2.81 us

profile of v1, /device:TPU:32, one launch (start us, length us, event | category | flops | bytes accessed | tf_op | source)
XLA Modules:
  0.0 59.7 jit_solution(4201886154288666621)
XLA Ops:
  0.0 0.0 copy-start.1
  0.0 0.7 %copy-done.1 = s32[1,32,1]{1,2,0:T(1,128)S(1)} copy-done((s32[1,32,1]{1,2,0:T(1,128)S(1)}, s32[1,32,1]{1,2,0:T(1,128)}, u32[]{:S(2)}) %copy-start.1) | copy-done | bytes 152
  0.7 0.2 convert_reduce_fusion
  0.8 0.0 copy-start
  0.9 0.7 %select_reduce_fusion.inv = s32[64]{0:T(128)} fusion(s32[32]{0:T(128)S(1)} %get-tuple-element.9, s32[32]{0:T(128)S(1)} %get-tuple-element.10), kind=kLoop, calls=%fused_computation | loop fusion | flops 6080 | bytes 512 | tf_op jit(solution)/shard_map/reduce_sum | solution.py:567
  1.5 0.0 copy-done
  1.5 0.7 %copy.10.offset = s32[16,2]{1,0:T(8,128)} copy(s32[16,2]{0,1:T(2,128)S(1)} %copy-done) | data formatting | bytes 256 | tf_op args[7]
  2.2 21.8 %exchange.1 = (f32[768,128]{1,0:T(8,128)}, s32[64,128]{1,0:T(8,128)}) custom-call(s32[64]{0:T(128)} %select_reduce_fusion.inv, s32[32]{0:T(128)} %bitcast.10, s32[32]{0:T(128)} %bitcast.11, f32[32,8,128]{2,1,0:T(8,128)} %bitcast.7, f32[32,2,128]{2,1,0:T(2,128)} %bitcast.8, f32[32,128]{1,0:T(8,128)} %bitcast.9), custom_call_target="tpu_custom_call" | custom-call | tf_op jit(solution)/shard_map/exchange/pallas_call | solution.py:150
  24.0 24.4 %grid_tile.1.tile = f32[8,128,128]{2,1,0:T(8,128)} custom-call(s32[64,128]{1,0:T(8,128)} %get-tuple-element.7.info, s32[16,2]{1,0:T(8,128)} %copy.10.offset, f32[32,32]{1,0:T(8,128)} %taper.1, f32[768,128]{1,0:T(8,128)} %get-tuple-element.8.got), custom_call_target="tpu_custom_call" | custom-call | tf_op jit(solution)/shard_map/grid_tile/pallas_call | solution.py:485
  48.5 9.7 %sum_over_freq.1 = f32[16,8,128]{2,1,0:T(8,128)} custom-call(f32[8,128,128]{2,1,0:T(8,128)} %grid_tile.1.tile), custom_call_target="tpu_custom_call" | custom-call | tf_op jit(solution)/shard_map/sum_over_freq/pallas_call | solution.py:544
  58.2 1.5 %copy.12 = f32[16,8,128]{2,1,0:T(8,128)} copy(f32[16,8,128]{2,1,0:T(8,128)} %sum_over_freq.1) | data formatting | bytes 131072
  (1 shorter events, 0.0 us)
Async XLA Ops:
  0.0 0.7 %copy-start.1 = (s32[1,32,1]{1,2,0:T(1,128)S(1)}, s32[1,32,1]{1,2,0:T(1,128)}, u32[]{:S(2)}) copy-start(s32[1,32,1]{1,2,0:T(1,128)} %param.13) | copy-start | bytes 388
  0.8 0.7 %copy-start = (s32[16,2]{0,1:T(2,128)S(1)}, s32[16,2]{0,1:T(2,128)}, u32[]{:S(2)}) copy-start(s32[16,2]{0,1:T(2,128)} %param.15) | copy-start | bytes 388

commit v2 on v1

--- a/solution.py
+++ b/solution.py
@@ -26,12 +26,11 @@
     0.10982451642699691,
 )
 COS_POLY = (
-    1.4142135620618328,
-    -6.97886410988463,
-    5.7398815391730755,
-    -1.8882749233647587,
-    0.3322515355413188,
-    -0.03450161282339655,
+    1.4142134962552289,
+    -6.978850948563853,
+    5.7394603769076955,
+    -1.8835579059892091,
+    0.31068802753070307,
 )
 
 
@@ -68,41 +67,62 @@
     return lax.broadcasted_iota(jnp.int32, shape, axis)
 
 
+def partner(me, i, sign):
+    j = i // 4
+    dz = jnp.where(j % 2 == 0, 4 + j // 2, 4 - (j + 1) // 2)
+    dy = 1 - (i % 4) // 2
+    dc = 1 - i % 2
+    y = (me // 16 + dy) % 2
+    z = (me // 2 + 8 + sign * dz) % 8
+    return y * 16 + z * 2 + (me + dc) % 2
+
+
 def exchange_kernel(
-    inv, slot, count, vis, uvo, wo, got, info, send, recv, send_sem, recv_sem
+    owner, slot, count, vis, uvo, wo, got, info, send, recv, send_sem, recv_sem
 ):
     me = lax.axis_index("uv")
     barrier = pltpu.get_barrier_semaphore()
 
     def greet(k, carry):
-        peer = lax.rem(me + k, OWNERS)
+        peer = partner(me, k, 1)
         pl.semaphore_signal(
             barrier, inc=1, device_id={"uv": peer}, device_id_type=pl.DeviceIdType.MESH
         )
         return carry
 
-    lax.fori_loop(1, OWNERS, greet, 0)
-
-    lane = iota((1, BLK), 1)
-
-    def pack(o, carry):
-        others = []
-        for rank in range(2):
-            entry = inv[2 * o + rank]
-            used = entry > 0
-            j = jnp.maximum(entry - 1, 0)
-            send[pl.ds(o * ROWS + 8 * rank, 8), :] = jnp.where(used, vis[j], 0.0)
-            live = jnp.where(used, count[j], 0)
-            facts = jnp.where(lane == 0, slot[j], live).astype(jnp.float32)
-            others += [uvo[j], wo[pl.ds(j, 1), :], facts]
-        send[pl.ds(o * ROWS + 16, 8), :] = jnp.concatenate(others, 0)
-        return carry
-
-    lax.fori_loop(0, OWNERS, pack, 0)
+    lax.fori_loop(0, OWNERS - 1, greet, 0)
+
+    size = vis.shape[0]
+    mine = owner[...].astype(jnp.float32)
+    across = jnp.broadcast_to(mine, (size, size))
+    row, col = iota((size, size), 0), iota((size, size), 1)
+    down = jnp.sum(jnp.where(row == col, across, 0.0), axis=1, keepdims=True)
+    earlier = jnp.where((down == across) & (row < col), 1.0, 0.0)
+    target = mine + OWNERS * jnp.sum(earlier, axis=0, keepdims=True)
+    pick = jnp.where(iota((SLOTS, size), 0).astype(jnp.float32) == target, 1.0, 0.0)
+    slots = jnp.sum(pick * slot[...].astype(jnp.float32), axis=1, keepdims=True)
+    counts = jnp.sum(pick * count[...].astype(jnp.float32), axis=1, keepdims=True)
+    lane = iota((SLOTS, BLK), 1)
+    facts = jnp.where(lane == 0, slots, jnp.where(lane == 1, counts, 0.0))
+    data = jnp.concatenate(
+        [vis[:, c, :] for c in range(8)] + [uvo[:, 0, :], uvo[:, 1, :], wo[...]], 1
+    )
+    hi = data.astype(jnp.bfloat16)
+    rest = data - hi.astype(jnp.float32)
+    mid, lo = split(rest)
+    pick = pick.astype(jnp.bfloat16)
+    moved = dot_nn(jnp.concatenate([pick] * 3, 1), jnp.concatenate([hi, mid, lo], 0))
+    for rank in range(2):
+        part = slice(rank * OWNERS, rank * OWNERS + OWNERS)
+        for c in range(12):
+            value = moved[part, c * BLK : c * BLK + BLK] if c < 11 else facts[part, :]
+            at = 8 * rank + c if c < 8 else 16 + 4 * rank + c - 8
+            send[pl.ds(at, OWNERS, stride=ROWS), :] = value
+
     pl.semaphore_wait(barrier, OWNERS - 1)
 
     def copy_to(k):
-        peer = lax.rem(me + k, OWNERS)
+        peer = partner(me, k, 1)
         return pltpu.make_async_remote_copy(
             src_ref=send.at[pl.ds(pl.multiple_of(peer * ROWS, 8), ROWS)],
             dst_ref=recv.at[pl.ds(pl.multiple_of(me * ROWS, 8), ROWS)],
@@ -116,12 +136,12 @@
         copy_to(k).start()
         return carry
 
-    lax.fori_loop(1, OWNERS, start, 0)
+    lax.fori_loop(0, OWNERS - 1, start, 0)
     own = pl.ds(pl.multiple_of(me * ROWS, 8), ROWS)
     recv[own, :] = send[own, :]
 
     def finish(k, carry):
-        source = lax.rem(me + OWNERS - k, OWNERS)
+        source = partner(me, k, -1)
         pltpu.make_async_remote_copy(
             src_ref=send.at[pl.ds(pl.multiple_of(source * ROWS, 8), ROWS)],
             dst_ref=recv.at[pl.ds(pl.multiple_of(source * ROWS, 8), ROWS)],
@@ -132,28 +152,31 @@
         ).wait_recv()
         return carry
 
-    lax.fori_loop(1, OWNERS, finish, 0)
+    lax.fori_loop(0, OWNERS - 1, finish, 0)
     got[...] = recv[...]
-    info[0:OWNERS, :] = recv[pl.ds(19, OWNERS, stride=ROWS), :].astype(jnp.int32)
-    info[OWNERS:, :] = recv[pl.ds(23, OWNERS, stride=ROWS), :].astype(jnp.int32)
+    known = jnp.concatenate(
+        [recv[pl.ds(19, OWNERS, stride=ROWS), :], recv[pl.ds(23, OWNERS, stride=ROWS), :]]
+        + [jnp.zeros((BLK - SLOTS, BLK), jnp.float32)],
+        0,
+    )
+    info[...] = jnp.transpose(known)[0:8, :].astype(jnp.int32)
 
     def drain(k, carry):
         copy_to(k).wait_send()
         return carry
 
-    lax.fori_loop(1, OWNERS, drain, 0)
-
-
-def exchange(inv, slot, count, vis, uvo, wo):
-    smem = pl.BlockSpec(memory_space=pltpu.SMEM)
+    lax.fori_loop(0, OWNERS - 1, drain, 0)
+
+
+def exchange(owner, slot, count, vis, uvo, wo):
     vmem = pl.BlockSpec(memory_space=pltpu.VMEM)
     return pl.pallas_call(
         exchange_kernel,
         out_shape=(
             jax.ShapeDtypeStruct((OWNERS * ROWS, BLK), jnp.float32),
-            jax.ShapeDtypeStruct((SLOTS, BLK), jnp.int32),
+            jax.ShapeDtypeStruct((8, BLK), jnp.int32),
         ),
-        in_specs=[smem] * 3 + [vmem] * 3,
+        in_specs=[vmem] * 6,
         out_specs=(vmem, vmem),
         scratch_shapes=[
             pltpu.VMEM((OWNERS * ROWS, BLK), jnp.float32),
@@ -161,9 +184,11 @@
             pltpu.SemaphoreType.DMA((OWNERS,)),
             pltpu.SemaphoreType.DMA((OWNERS,)),
         ],
-        compiler_params=pltpu.CompilerParams(collective_id=0, has_side_effects=True),
+        compiler_params=pltpu.CompilerParams(
+            collective_id=0, has_side_effects=True, vmem_limit_bytes=62 * 1024 * 1024
+        ),
         name="exchange",
-    )(inv, slot, count, vis, uvo, wo)
+    )(owner, slot, count, vis, uvo, wo)
 
 
 N_PHASE = 216
@@ -172,7 +197,8 @@
 ROW_M = 208
 ROW_U = 216
 ROW_V = 232
-N_TRIG = 248
+ROW_E = 248
+N_TRIG = 272
 TILE_A = (tuple(range(8)) + (16,), tuple(range(8, 16)))
 C_ROWS = (0, 9 * 32, 17 * 32)
 
@@ -209,11 +235,12 @@
         if t == 0:
             c16 = jnp.where(first_row, cosines[ROW_M + 1 : ROW_M + 2, :], 0.0)
             sv = jnp.where(first_row, -sines[ROW_M + 1 : ROW_M + 2, :], sv)
+        less = -sv
         for c in range(8):
             one = jnp.broadcast_to(vis[c : c + 1, :], (8, BLK))
             two = jnp.broadcast_to(swapped[c : c + 1, :], (8, BLK))
             at = t * 128 + c * 16
-            left, right = two * sv, -(one * sv)
+            left, right = two * sv, one * less
             if t == 0:
                 left, right = left + one * c16, right + two * c16
             d_part[at : at + 8, 0:BLK] = one * cv
@@ -225,29 +252,33 @@
     cu1 = cosines[ROW_U + 8 : ROW_U + 16, :]
     su0 = sines[ROW_U : ROW_U + 8, :]
     su1 = sines[ROW_U + 8 : ROW_U + 16, :]
-    cu2 = jnp.where(first_row, cosines[ROW_M : ROW_M + 1, :], cu0)
-    su2 = jnp.where(first_row, sines[ROW_M : ROW_M + 1, :], su0)
+    c16 = cosines[ROW_M : ROW_M + 1, :]
+    s16 = sines[ROW_M : ROW_M + 1, :]
+    for at, to in ((ROW_C, ROW_E), (ROW_C + 8, ROW_E + 8), (ROW_M, ROW_E + 16)):
+        c, s = cosines[at : at + 8, :], sines[at : at + 8, :]
+        cosines[to : to + 8, :] = c * c16 + s * s16
+        sines[to : to + 8, :] = s * c16 - c * s16
     for t in range(2):
         for i, a in enumerate(TILE_A[t]):
+            edge = slice(ROW_E + a, ROW_E + a + 1)
             if a < 8:
                 p0 = slice(a * 8, a * 8 + 8)
                 p1 = pl.ds(ROW_B + a, 8, stride=16)
-                edge = slice(ROW_C + a, ROW_C + a + 1)
             elif a < 16:
                 p0 = slice(ROW_B + (a - 8) * 16, ROW_B + (a - 8) * 16 + 8)
                 p1 = slice(ROW_B + (a - 8) * 16 + 8, ROW_B + (a - 8) * 16 + 16)
-                edge = slice(ROW_C + a, ROW_C + a + 1)
             else:
                 p0 = slice(ROW_C, ROW_C + 8)
                 p1 = slice(ROW_C + 8, ROW_C + 16)
-                edge = slice(ROW_M + 2, ROW_M + 3)
+                edge = slice(ROW_E + 18, ROW_E + 19)
             cw0, sw0 = cosines[p0, :], sines[p0, :]
             cw1, sw1 = cosines[p1, :], sines[p1, :]
-            cw2 = jnp.where(first_row, cosines[edge, :], cw0)
-            sw2 = jnp.where(first_row, sines[edge, :], sw0)
-            cc, ss, sc, cs = cw1 * cu1, sw1 * su1, sw1 * cu1, cw1 * su1
-            cos_rows = [cw0 * cu0 - sw0 * su0, cc - ss, cw2 * cu2 + sw2 * su2, cc + ss]
-            sin_rows = [sw0 * cu0 + cw0 * su0, sc + cs, sw2 * cu2 - cw2 * su2, sc - cs]
+            cc0, ss0, sc0, cs0 = cw0 * cu0, sw0 * su0, sw0 * cu0, cw0 * su0
+            cc1, ss1, sc1, cs1 = cw1 * cu1, sw1 * su1, sw1 * cu1, cw1 * su1
+            cos_2 = jnp.where(first_row, cosines[edge, :], cc0 + ss0)
+            sin_2 = jnp.where(first_row, sines[edge, :], sc0 - cs0)
+            cos_rows = [cc0 - ss0, cc1 - ss1, cos_2, cc1 + ss1]
+            sin_rows = [sc0 + cs0, sc1 + cs1, sin_2, sc1 - cs1]
             at = C_ROWS[t] + i * 32
             for part, rows in enumerate((cos_rows, sin_rows)):
                 for k in range(4):
@@ -304,8 +335,8 @@
     lax.fori_loop(0, OWNED, clear_total, 0)
 
     def add_total(b, carry):
-        s = info[b, 0]
-        total[s] = total[s] + info[b, 1]
+        s = info[0, b]
+        total[s] = total[s] + info[1, b]
         return carry
 
     lax.fori_loop(0, SLOTS, add_total, 0)
@@ -339,8 +370,8 @@
             others = got[pl.ds(i * ROWS + 16, 8), :]
             for rank in range(2):
                 b = i + OWNERS * rank
-                s = info[b, 0]
-                n = info[b, 1]
+                s = info[0, b]
+                n = info[1, b]
                 at = base[s]
                 base[s] = at + n
                 g = lax.shift_right_logical(at, 7)
@@ -413,14 +444,19 @@
         1.0 / math.sqrt(BLK)
     )
 
-    xr = x_of(iota((SUB, BLK), 0))
-    kx = iota((SUB, BLK), 1)
-    sx, cx = sincos_turns((xr * kx & (SUB - 1)).astype(jnp.float32) * (1.0 / SUB))
-    table_re = jnp.where(kx < SUB, cx * (1.0 / SUB), 0.0)
-    table_im = jnp.where(kx < SUB, sx * (-1.0 / SUB), 0.0)
+    row, col = iota((BLK, BLK), 0), iota((BLK, BLK), 1)
+    turn = (x_of(row & (SUB - 1)) * (col & (SUB - 1))) & (SUB - 1)
+    sx, cx = sincos_turns(turn.astype(jnp.float32) * (1.0 / SUB))
+    same = lax.shift_right_logical(row, 5) == lax.shift_right_logical(col, 5)
+    w_hi, w_lo = split(
+        jnp.concatenate(
+            [jnp.where(same, cx * (1.0 / SUB), 0.0), jnp.where(same, sx * (-1.0 / SUB), 0.0)], 1
+        )
+    )
+    w_all = jnp.concatenate([w_hi, w_hi, w_lo], 0)
     lane = iota((SUB, BLK), 1)
     even_lane = (lane & 8) == 0
-    nothing = jnp.zeros((SUB, 2 * BLK), jnp.bfloat16)
+    lane16 = iota((16, BLK), 1)
 
     for q in range(OWNED // 4):
         rows = []
@@ -433,41 +469,37 @@
                     y = jnp.where((lane & 7) == 0, a, y)
                 both.append(y)
             rows.append(jnp.concatenate(both, 1) * weight)
-        image = jnp.transpose(jnp.concatenate(rows, 0))
-        x_hi, x_lo = split(image)
-        x_both = jnp.concatenate([x_hi, x_lo], 1)
-        for j in range(4):
-            s = 4 * q + j
-            right = offset[s, 1]
-            t_hi, t_lo = split(
-                jnp.concatenate(
-                    [pltpu.roll(table_re, right, 1), pltpu.roll(table_im, right, 1)], 1
-                )
-            )
-            w_hi = jnp.concatenate([nothing] * j + [t_hi] + [nothing] * (3 - j), 0)
-            w_lo = jnp.concatenate([nothing] * j + [t_lo] + [nothing] * (3 - j), 0)
-            z = dot_nn(x_both, jnp.concatenate([w_hi, w_hi], 0)) + dot_nn(x_hi, w_lo)
-            for t in range(2):
-                for p in range(4):
-                    re = z[t * 128 + p * 16 : t * 128 + p * 16 + 16, :]
-                    im = z[t * 128 + p * 16 + 64 : t * 128 + p * 16 + 80, :]
-                    at = s * SUB + t * 16
-                    spread[p, at : at + 16, 0:BLK] = re[:, 0:BLK] - im[:, BLK:]
-                    spread[p, at : at + 16, BLK:] = re[:, BLK:] + im[:, 0:BLK]
+        x_hi, x_lo = split(jnp.transpose(jnp.concatenate(rows, 0)))
+        z = dot_nn(jnp.concatenate([x_hi, x_lo, x_hi], 1), w_all)
+        rights = [offset[1, 4 * q + j] for j in range(4)]
+        inside = [(lane16 >= right) & (lane16 < right + SUB) for right in rights]
+        for t in range(2):
+            for p in range(4):
+                re = z[t * 128 + p * 16 : t * 128 + p * 16 + 16, :]
+                im = z[t * 128 + p * 16 + 64 : t * 128 + p * 16 + 80, :]
+                joined = (re[:, 0:BLK] - im[:, BLK:], re[:, BLK:] + im[:, 0:BLK])
+                for j in range(4):
+                    at = (4 * q + j) * SUB + t * 16
+                    shift = (rights[j] + (BLK - SUB * j)) & (BLK - 1)
+                    for part in range(2):
+                        spread[p, at : at + 16, part * BLK : part * BLK + BLK] = jnp.where(
+                            inside[j], pltpu.roll(joined[part], shift, 1), 0.0
+                        )
 
     lane = iota((1, OWNED * SUB), 1)
     corner = jnp.zeros((1, OWNED * SUB), jnp.int32)
     for s in range(OWNED):
-        corner = jnp.where(lax.shift_right_logical(lane, 5) == s, offset[s, 0], corner)
+        corner = jnp.where(lax.shift_right_logical(lane, 5) == s, offset[0, s], corner)
     ky = iota((TILE, OWNED * SUB), 0) - corner
     yy = y_of(lax.shift_right_logical(lane, 4) & 1, lax.shift_right_logical(lane, 3) & 1, lane & 7)
     sy, cy = sincos_turns(((ky * yy) & (SUB - 1)).astype(jnp.float32) * (1.0 / SUB))
     inside = (ky >= 0) & (ky < SUB)
     h = jnp.concatenate([jnp.where(inside, cy, 0.0), jnp.where(inside, -sy, 0.0)], 0)
     h_hi, h_lo = split(h)
+    h_all = jnp.concatenate([h_hi, h_hi, h_lo], 1)
     for p in range(4):
         b_hi, b_lo = split(spread[p])
-        o = dot_nn(h_hi, b_hi) + dot_nn(h_hi, b_lo) + dot_nn(h_lo, b_hi)
+        o = dot_nn(h_all, jnp.concatenate([b_hi, b_lo, b_hi], 0))
         tile[p] = o[0:TILE, 0:BLK] - o[TILE:, BLK:]
         tile[p + 4] = o[0:TILE, BLK:] + o[TILE:, 0:BLK]
 
@@ -503,21 +535,28 @@
     )(info, offset, taper, got)
 
 
+FAR_FIRST = (6, 5, 7, 2, 4, 1, 3)
+
+
+def near(me, k, sign):
+    return (me // 4 + k // 4) % 2 * 4 + (me + 4 + sign * (k % 4)) % 4
+
+
 def sum_kernel(tile, out, recv, send_sem, recv_sem):
     me = lax.axis_index("freq")
     barrier = pltpu.get_barrier_semaphore()
-    for k in range(1, GROUPS):
+    for k in FAR_FIRST:
         pl.semaphore_signal(
             barrier,
             inc=1,
-            device_id={"freq": lax.rem(me + k, GROUPS)},
+            device_id={"freq": near(me, k, 1)},
             device_id_type=pl.DeviceIdType.MESH,
         )
     pl.semaphore_wait(barrier, GROUPS - 1)
     strip = TILE // GROUPS
     copies = []
-    for k in range(1, GROUPS):
-        peer = lax.rem(me + k, GROUPS)
+    for k in FAR_FIRST:
+        peer = near(me, k, 1)
         copy = pltpu.make_async_remote_copy(
             src_ref=tile.at[:, pl.ds(pl.multiple_of(peer * strip, 8), strip)],
             dst_ref=recv.at[k],
@@ -529,8 +568,8 @@
         copy.start()
         copies.append(copy)
     value = tile[:, pl.ds(pl.multiple_of(me * strip, 8), strip), :]
-    for k in range(1, GROUPS):
-        copies[k - 1].wait_recv()
+    for k, copy in zip(FAR_FIRST, copies):
+        copy.wait_recv()
         value = value + recv[k]
     for c in range(8):
         out[:, c, :] = value[c]
@@ -551,7 +590,9 @@
             pltpu.SemaphoreType.DMA((GROUPS,)),
             pltpu.SemaphoreType.DMA((GROUPS,)),
         ],
-        compiler_params=pltpu.CompilerParams(collective_id=1, has_side_effects=True),
+        compiler_params=pltpu.CompilerParams(
+            collective_id=1, has_side_effects=True, vmem_limit_bytes=62 * 1024 * 1024
+        ),
         name="sum_over_freq",
     )(tile)
 
@@ -559,21 +600,10 @@
 def shards(
     visibility, uv_offset, w_offset, taper, row_count, block_owner, block_slot, subgrid_offset
 ):
-    owner = block_owner[0, :, 0]
-    blocks = owner.shape[0]
-    index = jnp.arange(blocks, dtype=jnp.int32)
-    same = (owner[:, None] == owner[None, :]) & (index[None, :] < index[:, None])
-    target = 2 * owner + jnp.sum(same.astype(jnp.int32), axis=1)
-    inv = jnp.sum(
-        jnp.where(
-            target[None, :] == jnp.arange(SLOTS, dtype=jnp.int32)[:, None], index[None, :] + 1, 0
-        ),
-        axis=1,
-    )
     got, info = exchange(
-        inv, block_slot[0], row_count[0], visibility[0], uv_offset[0], w_offset[0]
-    )
-    return sum_over_freq(grid_tile(info, subgrid_offset, taper, got))
+        block_owner[:, :, 0], block_slot, row_count, visibility[0], uv_offset[0], w_offset[0]
+    )
+    return sum_over_freq(grid_tile(info, subgrid_offset.T, taper, got))
 
 
 def solution(mesh):

time: 60 us -> 56.7 us (0.945)
  local copies, waits for them, and re-layouts: 2.81 us -> 1.47 us
  Pallas kernels: 56 us -> 55 us
  other arithmetic: 0.87 us -> 0 us
    pallas_call x1, Pallas kernels: 24.4 us -> 20.2 us  [grid_tile(): pl.pallas_call(grid_kernel, out_shape=jax.ShapeDtypeStruct((8, TILE, TILE...]
    pallas_call x1, Pallas kernels: 9.74 us -> 13 us  [sum_over_freq(): pl.pallas_call(sum_kernel, out_shape=jax.ShapeDtypeStruct((strip, 8, TILE...]
    unnamed x6 -> x1, local copies, waits for them, and re-layouts: 2.81 us -> 1.47 us
    reduce_sum x2 -> x0, other arithmetic: 0.86 us -> none  [the longest x1 0.68 us: shards(): jnp.sum(jnp.where(target[None, :] == jnp.arange(SLOTS, dtype=jnp.int32)[:...]
where the time goes in v2:
time: 56.7 us; the launch traced here: 56.5 us
  Pallas kernels  55 us (97%)
  local copies, waits for them, and re-layouts  1.47 us (3%)
    pallas_call x1, Pallas kernels, exchange(): pl.pallas_call(exchange_kernel, out_shape=(jax.ShapeDtypeStruct((OWNERS *...  21.8 us
    pallas_call x1, Pallas kernels, grid_tile(): pl.pallas_call(grid_kernel, out_shape=jax.ShapeDtypeStruct((8, TILE, TILE...  20.2 us
    pallas_call x1, Pallas kernels, sum_over_freq(): pl.pallas_call(sum_kernel, out_shape=jax.ShapeDtypeStruct((strip, 8, TILE...  13 us
    unnamed x1, local copies, waits for them, and re-layouts  1.47 us

profile of v2, /device:TPU:32, one launch (start us, length us, event | category | flops | bytes accessed | tf_op | source)
XLA Modules:
  0.0 56.5 jit_solution(16507231636146880634)
XLA Ops:
  0.0 21.8 %exchange.1 = (f32[768,128]{1,0:T(8,128)}, s32[8,128]{1,0:T(8,128)}) custom-call(s32[1,32]{1,0:T(1,128)} %bitcast.9, s32[1,32]{1,0:T(1,128)} %slot.1, s32[1,32]{1,0:T(1,128)} %count.1, f32[32,8,128]{2,1,0:T(8,128)} %bitcast.5, f32[32,2,128]{2,1,0:T(2,128)} %bitcast.6, f32[32,128]{1,0:T(8,128)} %bitcast.7), custom_call_target="tpu_custom_call" | custom-call | tf_op jit(solution)/shard_map/exchange/pallas_call | solution.py:173
  21.8 20.2 %grid_tile.1.tile = f32[8,128,128]{2,1,0:T(8,128)} custom-call(s32[8,128]{1,0:T(8,128)} %get-tuple-element.7.info, s32[2,16]{1,0:T(2,128)} %bitcast.8, f32[32,32]{1,0:T(8,128)} %taper.1, f32[768,128]{1,0:T(8,128)} %get-tuple-element.8.got), custom_call_target="tpu_custom_call" | custom-call | tf_op jit(solution)/shard_map/grid_tile/pallas_call | solution.py:517
  42.0 13.0 %sum_over_freq.1 = f32[16,8,128]{2,1,0:T(8,128)} custom-call(f32[8,128,128]{2,1,0:T(8,128)} %grid_tile.1.tile), custom_call_target="tpu_custom_call" | custom-call | tf_op jit(solution)/shard_map/sum_over_freq/pallas_call | solution.py:583
  55.0 1.5 %copy.10 = f32[16,8,128]{2,1,0:T(8,128)} copy(f32[16,8,128]{2,1,0:T(8,128)} %sum_over_freq.1) | data formatting | bytes 131072

commit v3 on v2

--- a/solution.py
+++ b/solution.py
@@ -159,7 +159,10 @@
         + [jnp.zeros((BLK - SLOTS, BLK), jnp.float32)],
         0,
     )
-    info[...] = jnp.transpose(known)[0:8, :].astype(jnp.int32)
+    own_slot = iota((BLK, BLK), 1).astype(jnp.float32) == known[:, 0:1]
+    totals = jnp.sum(jnp.where(own_slot, known[:, 1:2], 0.0), axis=0, keepdims=True)
+    listed = jnp.transpose(known)[0:8, :]
+    info[...] = jnp.where(iota((8, BLK), 0) == 2, totals, listed).astype(jnp.int32)
 
     def drain(k, carry):
         copy_to(k).wait_send()
@@ -191,14 +194,28 @@
     )(owner, slot, count, vis, uvo, wo)
 
 
-N_PHASE = 216
+ROW_L = 0
 ROW_B = 64
+ROW_H = 128
 ROW_C = 192
 ROW_M = 208
 ROW_U = 216
 ROW_V = 232
 ROW_E = 248
 N_TRIG = 272
+N_ONCE = 72
+N_PHASE = 160
+
+
+def once(k):
+    if k < 6:
+        base, k = (ROW_L, ROW_H)[k // 3], k % 3 + 1
+        return ((0, 8 - k, base, 8 - k, 0), (8 - k, k, base, k, 0))
+    if k == 6:
+        return ((0, 4, ROW_L, 4, 0), (4, 4, ROW_H, 4, 0))
+    return ((0, 8, (ROW_L, ROW_H)[k - 7], 0, 1),)
+
+
 TILE_A = (tuple(range(8)) + (16,), tuple(range(8, 16)))
 C_ROWS = (0, 9 * 32, 17 * 32)
 
@@ -219,13 +236,25 @@
         sines[at : at + 8, :] = s
         cosines[at : at + 8, :] = c
 
-    keep(ROW_M, jnp.where(sub == 0, u, jnp.where(sub == 1, v, w)) * ntab[ROW_M : ROW_M + 8, :])
+    keep(ROW_M, jnp.where(sub == 0, u, jnp.where(sub == 1, v, w)) * ntab[152:160, :])
     keep(ROW_U, u * step0)
     keep(ROW_U + 8, u * step1)
     keep(ROW_V, v * step0)
     keep(ROW_V + 8, v * step1)
-    for at in range(0, ROW_M, 8):
-        keep(at, w * ntab[at : at + 8, :])
+    for k in range(N_ONCE // 8):
+        s, c = sincos_turns(w * ntab[8 * k : 8 * k + 8, :])
+        for first, size, base, a, diagonal in once(k):
+            for table, value in ((sines, s), (cosines, c)):
+                part = value[first : first + size, :]
+                if diagonal:
+                    table[pl.ds(base, size, stride=9), :] = part
+                else:
+                    table[base + a * 8 : base + a * 8 + size, :] = part
+                    table[pl.ds(base + a, size, stride=8), :] = part
+    for k in range(8):
+        keep(ROW_B + 8 * k, w * ntab[N_ONCE + 8 * k : N_ONCE + 8 * k + 8, :])
+    keep(ROW_C, w * ntab[136:144, :])
+    keep(ROW_C + 8, w * ntab[144:152, :])
 
     vis = buf[g, 0:8, :]
     swapped = pltpu.roll(vis, 4, 0) * halves
@@ -262,23 +291,21 @@
         for i, a in enumerate(TILE_A[t]):
             edge = slice(ROW_E + a, ROW_E + a + 1)
             if a < 8:
-                p0 = slice(a * 8, a * 8 + 8)
-                p1 = pl.ds(ROW_B + a, 8, stride=16)
+                p0 = slice(ROW_L + a * 8, ROW_L + a * 8 + 8)
+                p1 = pl.ds(ROW_B + a, 8, stride=8)
             elif a < 16:
-                p0 = slice(ROW_B + (a - 8) * 16, ROW_B + (a - 8) * 16 + 8)
-                p1 = slice(ROW_B + (a - 8) * 16 + 8, ROW_B + (a - 8) * 16 + 16)
+                p0 = slice(ROW_B + (a - 8) * 8, ROW_B + (a - 8) * 8 + 8)
+                p1 = slice(ROW_H + (a - 8) * 8, ROW_H + (a - 8) * 8 + 8)
             else:
                 p0 = slice(ROW_C, ROW_C + 8)
                 p1 = slice(ROW_C + 8, ROW_C + 16)
                 edge = slice(ROW_E + 18, ROW_E + 19)
             cw0, sw0 = cosines[p0, :], sines[p0, :]
             cw1, sw1 = cosines[p1, :], sines[p1, :]
-            cc0, ss0, sc0, cs0 = cw0 * cu0, sw0 * su0, sw0 * cu0, cw0 * su0
-            cc1, ss1, sc1, cs1 = cw1 * cu1, sw1 * su1, sw1 * cu1, cw1 * su1
-            cos_2 = jnp.where(first_row, cosines[edge, :], cc0 + ss0)
-            sin_2 = jnp.where(first_row, sines[edge, :], sc0 - cs0)
-            cos_rows = [cc0 - ss0, cc1 - ss1, cos_2, cc1 + ss1]
-            sin_rows = [sc0 + cs0, sc1 + cs1, sin_2, sc1 - cs1]
+            cos_2 = jnp.where(first_row, cosines[edge, :], cw0 * su0)
+            sin_2 = jnp.where(first_row, sines[edge, :], sw0 * su0)
+            cos_rows = [cw0 * cu0, cw1 * cu1, cos_2, cw1 * su1]
+            sin_rows = [sw0 * cu0, sw1 * cu1, sin_2, sw1 * su1]
             at = C_ROWS[t] + i * 32
             for part, rows in enumerate((cos_rows, sin_rows)):
                 for k in range(4):
@@ -312,7 +339,6 @@
     taper,
     got,
     tile,
-    total,
     base,
     slot_of,
     buf,
@@ -328,22 +354,10 @@
     acc,
     spread,
 ):
-    def clear_total(s, carry):
-        total[s] = 0
-        return carry
-
-    lax.fori_loop(0, OWNED, clear_total, 0)
-
-    def add_total(b, carry):
-        s = info[0, b]
-        total[s] = total[s] + info[1, b]
-        return carry
-
-    lax.fori_loop(0, SLOTS, add_total, 0)
     slot_of[0] = OWNED
 
     def place_slot(s, first):
-        number = lax.div(total[s] + (BLK - 1), BLK)
+        number = lax.shift_right_logical(info[2, s] + (BLK - 1), 7)
         base[s] = first * BLK
 
         def name_group(i, carry):
@@ -396,29 +410,44 @@
         return 1.0 - jnp.sqrt(1.0 - l * l - m * m)
 
     row = iota((8, BLK), 0).astype(jnp.float32)
-    for a in range(8):
-        ntab[a * 8 : a * 8 + 8, :] = n_of(float(a), row)
-    for a in range(8, 17):
-        for h in range(2):
-            at = ROW_B + (a - 8) * 16 + 8 * h
-            ntab[at : at + 8, :] = n_of(float(a), row + 8.0 * h)
-    ntab[ROW_M : ROW_M + 8, :] = jnp.where(
+    for k in range(N_ONCE // 8):
+        a, b = row, row
+        for first, size, base, y, diagonal in once(k):
+            shift = 0.0 if base == ROW_L else 8.0
+            here = row >= float(first)
+            a = jnp.where(here, row + shift if diagonal else float(y) + shift, a)
+            b = jnp.where(here, row - float(first) + shift, b)
+        ntab[8 * k : 8 * k + 8, :] = n_of(a, b)
+    for k in range(8):
+        ntab[N_ONCE + 8 * k : N_ONCE + 8 * k + 8, :] = n_of(float(8 + k), row)
+    ntab[136:144, :] = n_of(16.0, row)
+    ntab[144:152, :] = n_of(16.0, row + 8.0)
+    ntab[152:160, :] = jnp.where(
         row < 2.0, 16 * 0.5 / SUB, n_of(16.0, jnp.full((8, BLK), 16.0, jnp.float32))
     )
 
     for s in range(OWNED):
         acc[s] = jnp.zeros((2, SUB, BLK), jnp.float32)
 
-    def two_groups(i, carry):
-        g = 2 * i
+    def two_groups(g):
         phases(g, buf, ntab, sines_0, cosines_0, c_0, d_0)
         add_images(slot_of[g], c_1, d_1, acc)
         phases(g + 1, buf, ntab, sines_1, cosines_1, c_1, d_1)
         add_images(slot_of[g + 1], c_0, d_0, acc)
-        return carry
-
+
+    def four_groups(i, carry):
+        two_groups(4 * i)
+        two_groups(4 * i + 2)
+        return carry
+
+    def rest(i, carry):
+        two_groups(2 * i)
+        return carry
+
+    fours = lax.div(groups, 4)
     steps = lax.div(groups + 1, 2)
-    lax.fori_loop(0, steps, two_groups, 0)
+    lax.fori_loop(0, fours, four_groups, 0)
+    lax.fori_loop(2 * fours, steps, rest, 0)
     add_images(slot_of[2 * steps], c_1, d_1, acc)
 
     def y_of(high, sign, low):
@@ -457,6 +486,8 @@
     lane = iota((SUB, BLK), 1)
     even_lane = (lane & 8) == 0
     lane16 = iota((16, BLK), 1)
+    turn_sign = jnp.where(lane16 < BLK // 2, 1.0, -1.0)
+    edge = iota((16, BLK), 0) == 0
 
     for q in range(OWNED // 4):
         rows = []
@@ -467,7 +498,11 @@
                 y = jnp.where(even_lane, a + pltpu.roll(a, BLK - 8, 1), pltpu.roll(a, 8, 1) - a)
                 if t == 0:
                     y = jnp.where((lane & 7) == 0, a, y)
-                both.append(y)
+                cos_x, sin_x = y[0:16, :], y[16:32, :]
+                turned = pltpu.roll(sin_x, BLK // 2, 1) * turn_sign
+                plus = jnp.where(edge, cos_x, cos_x + turned)
+                minus = jnp.where(edge, sin_x, cos_x - turned)
+                both.append(jnp.concatenate([plus, minus], 0))
             rows.append(jnp.concatenate(both, 1) * weight)
         x_hi, x_lo = split(jnp.transpose(jnp.concatenate(rows, 0)))
         z = dot_nn(jnp.concatenate([x_hi, x_lo, x_hi], 1), w_all)
@@ -490,9 +525,17 @@
     corner = jnp.zeros((1, OWNED * SUB), jnp.int32)
     for s in range(OWNED):
         corner = jnp.where(lax.shift_right_logical(lane, 5) == s, offset[0, s], corner)
+    yy = y_of(lax.shift_right_logical(lane, 4) & 1, lax.shift_right_logical(lane, 3) & 1, lane & 7)
+
+    def turned(at, y):
+        return sincos_turns(((at * y) & (SUB - 1)).astype(jnp.float32) * (1.0 / SUB))
+
+    s_at, c_at = turned(iota((TILE, BLK), 0), jnp.broadcast_to(yy[:, 0:BLK], (TILE, BLK)))
+    s_at, c_at = jnp.concatenate([s_at] * 4, 1), jnp.concatenate([c_at] * 4, 1)
+    s_corner, c_corner = turned(corner, yy)
+    cy = c_at * c_corner + s_at * s_corner
+    sy = s_at * c_corner - c_at * s_corner
     ky = iota((TILE, OWNED * SUB), 0) - corner
-    yy = y_of(lax.shift_right_logical(lane, 4) & 1, lax.shift_right_logical(lane, 3) & 1, lane & 7)
-    sy, cy = sincos_turns(((ky * yy) & (SUB - 1)).astype(jnp.float32) * (1.0 / SUB))
     inside = (ky >= 0) & (ky < SUB)
     h = jnp.concatenate([jnp.where(inside, cy, 0.0), jnp.where(inside, -sy, 0.0)], 0)
     h_hi, h_lo = split(h)
@@ -521,7 +564,6 @@
         out_specs=vmem,
         scratch_shapes=[
             pltpu.SMEM((OWNED,), jnp.int32),
-            pltpu.SMEM((OWNED,), jnp.int32),
             pltpu.SMEM((MAX_GROUPS + 2,), jnp.int32),
             pltpu.VMEM((MAX_GROUPS, 16, BLK), f32),
             pltpu.VMEM((N_PHASE, BLK), f32),
@@ -542,8 +584,14 @@
     return (me // 4 + k // 4) % 2 * 4 + (me + 4 + sign * (k % 4)) % 4
 
 
-def sum_kernel(tile, out, recv, send_sem, recv_sem):
+def gather_kernel(tile, recv, send_sem, recv_sem):
     me = lax.axis_index("freq")
+    own = pltpu.make_async_copy(
+        tile.at[:, pl.ds(pl.multiple_of(me * (TILE // GROUPS), 8), TILE // GROUPS)],
+        recv.at[0],
+        recv_sem.at[0],
+    )
+    own.start()
     barrier = pltpu.get_barrier_semaphore()
     for k in FAR_FIRST:
         pl.semaphore_signal(
@@ -567,34 +615,47 @@
         )
         copy.start()
         copies.append(copy)
-    value = tile[:, pl.ds(pl.multiple_of(me * strip, 8), strip), :]
-    for k, copy in zip(FAR_FIRST, copies):
+    own.wait()
+    for copy in copies:
         copy.wait_recv()
-        value = value + recv[k]
+    for copy in copies:
+        copy.wait_send()
+
+
+def sum_kernel(parts, out):
+    value = parts[0]
+    for k in range(1, GROUPS):
+        value = value + parts[k]
     for c in range(8):
         out[:, c, :] = value[c]
-    for copy in copies:
-        copy.wait_send()
 
 
 def sum_over_freq(tile):
+    strip = TILE // GROUPS
+    anywhere = pl.BlockSpec(memory_space=pl.ANY)
     vmem = pl.BlockSpec(memory_space=pltpu.VMEM)
-    strip = TILE // GROUPS
-    return pl.pallas_call(
-        sum_kernel,
-        out_shape=jax.ShapeDtypeStruct((strip, 8, TILE), jnp.float32),
-        in_specs=[vmem],
-        out_specs=vmem,
+    parts = pl.pallas_call(
+        gather_kernel,
+        out_shape=jax.ShapeDtypeStruct((GROUPS, 8, strip, TILE), jnp.float32),
+        in_specs=[anywhere],
+        out_specs=anywhere,
         scratch_shapes=[
-            pltpu.VMEM((GROUPS, 8, strip, TILE), jnp.float32),
             pltpu.SemaphoreType.DMA((GROUPS,)),
             pltpu.SemaphoreType.DMA((GROUPS,)),
         ],
         compiler_params=pltpu.CompilerParams(
             collective_id=1, has_side_effects=True, vmem_limit_bytes=62 * 1024 * 1024
         ),
+        name="gather_over_freq",
+    )(tile)
+    return pl.pallas_call(
+        sum_kernel,
+        out_shape=jax.ShapeDtypeStruct((strip, 8, TILE), jnp.float32),
+        in_specs=[vmem],
+        out_specs=vmem,
+        compiler_params=pltpu.CompilerParams(vmem_limit_bytes=62 * 1024 * 1024),
         name="sum_over_freq",
-    )(tile)
+    )(parts)
 
 
 def shards(

time: 56.7 us -> 52.3 us (0.922)
  the two profiles are of different devices: /device:TPU:32 before, /device:TPU:33 now
where the time goes in v3:
time: 52.3 us; the launch traced here: 52.1 us
  Pallas kernels  52.1 us (100%)
    pallas_call x1, Pallas kernels, exchange(): pl.pallas_call(exchange_kernel, out_shape=(jax.ShapeDtypeStruct((OWNERS *...  22.1 us
    pallas_call x1, Pallas kernels, grid_tile(): pl.pallas_call(grid_kernel, out_shape=jax.ShapeDtypeStruct((8, TILE, TILE...  18 us
    pallas_call x1, Pallas kernels, sum_over_freq(): pl.pallas_call(gather_kernel, out_shape=jax.ShapeDtypeStruct((GROUPS, 8,...  10.3 us
    pallas_call x1, Pallas kernels, sum_over_freq(): pl.pallas_call(sum_kernel, out_shape=jax.ShapeDtypeStruct((strip, 8, TILE...  1.73 us

profile of v3, /device:TPU:33, one launch (start us, length us, event | category | flops | bytes accessed | tf_op | source)
XLA Modules:
  0.0 52.1 jit_solution(554668569267151473)
XLA Ops:
  0.0 22.1 %exchange.1 = (f32[768,128]{1,0:T(8,128)}, s32[8,128]{1,0:T(8,128)}) custom-call(s32[1,32]{1,0:T(1,128)} %bitcast.9, s32[1,32]{1,0:T(1,128)} %slot.1, s32[1,32]{1,0:T(1,128)} %count.1, f32[32,8,128]{2,1,0:T(8,128)} %bitcast.5, f32[32,2,128]{2,1,0:T(2,128)} %bitcast.6, f32[32,128]{1,0:T(8,128)} %bitcast.7), custom_call_target="tpu_custom_call" | custom-call | tf_op jit(solution)/shard_map/exchange/pallas_call | solution.py:176
  22.1 18.0 %grid_tile.1.tile = f32[8,128,128]{2,1,0:T(8,128)} custom-call(s32[8,128]{1,0:T(8,128)} %get-tuple-element.7.info, s32[2,16]{1,0:T(2,128)} %bitcast.8, f32[32,32]{1,0:T(8,128)} %taper.1, f32[768,128]{1,0:T(8,128)} %get-tuple-element.8.got), custom_call_target="tpu_custom_call" | custom-call | tf_op jit(solution)/shard_map/grid_tile/pallas_call | solution.py:560
  40.0 10.3 %gather_over_freq.1.parts = f32[8,8,16,128]{3,2,1,0:T(8,128)} custom-call(f32[8,128,128]{2,1,0:T(8,128)} %grid_tile.1.tile), custom_call_target="tpu_custom_call" | custom-call | tf_op jit(solution)/shard_map/gather_over_freq/pallas_call | solution.py:637
  50.4 1.7 %sum_over_freq.1 = f32[16,8,128]{2,1,0:T(8,128)} custom-call(f32[8,8,16,128]{3,2,1,0:T(8,128)} %gather_over_freq.1.parts), custom_call_target="tpu_custom_call" | custom-call | tf_op jit(solution)/shard_map/sum_over_freq/pallas_call | solution.py:651

commit v4 on v3

--- a/solution.py
+++ b/solution.py
@@ -264,18 +264,15 @@
         if t == 0:
             c16 = jnp.where(first_row, cosines[ROW_M + 1 : ROW_M + 2, :], 0.0)
             sv = jnp.where(first_row, -sines[ROW_M + 1 : ROW_M + 2, :], sv)
-        less = -sv
         for c in range(8):
             one = jnp.broadcast_to(vis[c : c + 1, :], (8, BLK))
             two = jnp.broadcast_to(swapped[c : c + 1, :], (8, BLK))
             at = t * 128 + c * 16
-            left, right = two * sv, one * less
+            odd = two * sv
             if t == 0:
-                left, right = left + one * c16, right + two * c16
-            d_part[at : at + 8, 0:BLK] = one * cv
-            d_part[at : at + 8, BLK:] = two * cv
-            d_part[at + 8 : at + 16, 0:BLK] = left
-            d_part[at + 8 : at + 16, BLK:] = right
+                odd = odd + one * c16
+            d_part[at : at + 8, :] = one * cv
+            d_part[at + 8 : at + 16, :] = odd
 
     cu0 = cosines[ROW_U : ROW_U + 8, :]
     cu1 = cosines[ROW_U + 8 : ROW_U + 16, :]
@@ -315,7 +312,13 @@
 def add_images(s, c_part, d_part, acc):
     lane = iota((SUB, BLK), 1)
     for t in range(2):
-        d_both = jnp.concatenate(split(d_part[t * 128 : t * 128 + 128, :]), 0)
+        d_both = jnp.concatenate(
+            [
+                jnp.concatenate([d, jnp.concatenate([d[64:, :], -d[:64, :]], 0)], 1)
+                for d in split(d_part[t * 128 : t * 128 + 128, :])
+            ],
+            0,
+        )
         c_hi, c_lo = split(c_part[C_ROWS[t] : C_ROWS[t + 1], :])
         o_hi = dot_nt(c_hi, d_both)
         o_lo = dot_nt(c_lo, d_both)
@@ -396,10 +399,10 @@
                 after = lane8 < shift + n - BLK
                 moved.append((g, vis, rest, here, after))
         for g, vis, rest, here, after in moved:
-            buf[g, 0:8, :] = jnp.where(here, vis, buf[g, 0:8, :])
-            buf[g, 8:16, :] = jnp.where(here, rest, buf[g, 8:16, :])
-            buf[g + 1, 0:8, :] = jnp.where(after, vis, buf[g + 1, 0:8, :])
-            buf[g + 1, 8:16, :] = jnp.where(after, rest, buf[g + 1, 8:16, :])
+            pltpu.store(buf.at[g, 0:8, :], vis, mask=here)
+            pltpu.store(buf.at[g, 8:16, :], rest, mask=here)
+            pltpu.store(buf.at[g + 1, 0:8, :], vis, mask=after)
+            pltpu.store(buf.at[g + 1, 8:16, :], rest, mask=after)
         return carry
 
     lax.fori_loop(0, OWNERS // 4, compact, 0)
@@ -555,7 +558,7 @@
         pltpu.VMEM((N_TRIG, BLK), f32),
         pltpu.VMEM((N_TRIG, BLK), f32),
         pltpu.VMEM((C_ROWS[2], 2 * BLK), f32),
-        pltpu.VMEM((256, 2 * BLK), f32),
+        pltpu.VMEM((256, BLK), f32),
     ]
     return pl.pallas_call(
         grid_kernel,

time: 52.3 us -> 48.9 us (0.935)
  the two profiles are of different devices: /device:TPU:33 before, /device:TPU:128 now
where the time goes in v4:
time: 48.9 us; the launch traced here: 48.8 us
  Pallas kernels  48.8 us (100%)
    pallas_call x1, Pallas kernels, exchange(): pl.pallas_call(exchange_kernel, out_shape=(jax.ShapeDtypeStruct((OWNERS *...  19.2 us
    pallas_call x1, Pallas kernels, grid_tile(): pl.pallas_call(grid_kernel, out_shape=jax.ShapeDtypeStruct((8, TILE, TILE...  17.3 us
    pallas_call x1, Pallas kernels, sum_over_freq(): pl.pallas_call(gather_kernel, out_shape=jax.ShapeDtypeStruct((GROUPS, 8,...  10.5 us
    pallas_call x1, Pallas kernels, sum_over_freq(): pl.pallas_call(sum_kernel, out_shape=jax.ShapeDtypeStruct((strip, 8, TILE...  1.73 us

profile of v4, /device:TPU:128, one launch (start us, length us, event | category | flops | bytes accessed | tf_op | source)
XLA Modules:
  0.0 48.8 jit_solution(853428904368748988)
XLA Ops:
  0.0 19.2 %exchange.1 = (f32[768,128]{1,0:T(8,128)}, s32[8,128]{1,0:T(8,128)}) custom-call(s32[1,32]{1,0:T(1,128)} %bitcast.9, s32[1,32]{1,0:T(1,128)} %slot.1, s32[1,32]{1,0:T(1,128)} %count.1, f32[32,8,128]{2,1,0:T(8,128)} %bitcast.5, f32[32,2,128]{2,1,0:T(2,128)} %bitcast.6, f32[32,128]{1,0:T(8,128)} %bitcast.7), custom_call_target="tpu_custom_call" | custom-call | tf_op jit(solution)/shard_map/exchange/pallas_call | solution.py:176
  19.2 17.3 %grid_tile.1.tile = f32[8,128,128]{2,1,0:T(8,128)} custom-call(s32[8,128]{1,0:T(8,128)} %get-tuple-element.7.info, s32[2,16]{1,0:T(2,128)} %bitcast.8, f32[32,32]{1,0:T(8,128)} %taper.1, f32[768,128]{1,0:T(8,128)} %get-tuple-element.8.got), custom_call_target="tpu_custom_call" | custom-call | tf_op jit(solution)/shard_map/grid_tile/pallas_call | solution.py:563
  36.5 10.5 %gather_over_freq.1.parts = f32[8,8,16,128]{3,2,1,0:T(8,128)} custom-call(f32[8,128,128]{2,1,0:T(8,128)} %grid_tile.1.tile), custom_call_target="tpu_custom_call" | custom-call | tf_op jit(solution)/shard_map/gather_over_freq/pallas_call | solution.py:640
  47.0 1.7 %sum_over_freq.1 = f32[16,8,128]{2,1,0:T(8,128)} custom-call(f32[8,8,16,128]{3,2,1,0:T(8,128)} %gather_over_freq.1.parts), custom_call_target="tpu_custom_call" | custom-call | tf_op jit(solution)/shard_map/sum_over_freq/pallas_call | solution.py:654

commit v5 on v4

--- a/solution.py
+++ b/solution.py
@@ -216,6 +216,7 @@
     return ((0, 8, (ROW_L, ROW_H)[k - 7], 0, 1),)
 
 
+STEP = 8
 TILE_A = (tuple(range(8)) + (16,), tuple(range(8, 16)))
 C_ROWS = (0, 9 * 32, 17 * 32)
 
@@ -438,19 +439,19 @@
         phases(g + 1, buf, ntab, sines_1, cosines_1, c_1, d_1)
         add_images(slot_of[g + 1], c_0, d_0, acc)
 
-    def four_groups(i, carry):
-        two_groups(4 * i)
-        two_groups(4 * i + 2)
+    def more_groups(i, carry):
+        for k in range(0, STEP, 2):
+            two_groups(STEP * i + k)
         return carry
 
     def rest(i, carry):
         two_groups(2 * i)
         return carry
 
-    fours = lax.div(groups, 4)
+    whole = lax.div(groups, STEP)
     steps = lax.div(groups + 1, 2)
-    lax.fori_loop(0, fours, four_groups, 0)
-    lax.fori_loop(2 * fours, steps, rest, 0)
+    lax.fori_loop(0, whole, more_groups, 0)
+    lax.fori_loop(STEP // 2 * whole, steps, rest, 0)
     add_images(slot_of[2 * steps], c_1, d_1, acc)
 
     def y_of(high, sign, low):
@@ -489,6 +490,7 @@
     lane = iota((SUB, BLK), 1)
     even_lane = (lane & 8) == 0
     lane16 = iota((16, BLK), 1)
+    first_row = iota((8, BLK), 0) == 0
     turn_sign = jnp.where(lane16 < BLK // 2, 1.0, -1.0)
     edge = iota((16, BLK), 0) == 0
 
@@ -515,7 +517,14 @@
             for p in range(4):
                 re = z[t * 128 + p * 16 : t * 128 + p * 16 + 16, :]
                 im = z[t * 128 + p * 16 + 64 : t * 128 + p * 16 + 80, :]
-                joined = (re[:, 0:BLK] - im[:, BLK:], re[:, BLK:] + im[:, 0:BLK])
+                re, im = re[:, 0:BLK] - im[:, BLK:], re[:, BLK:] + im[:, 0:BLK]
+                up, down = (re[:8], im[:8]), (re[8:], im[8:])
+                tops = [up[0] + down[0], up[1] + down[1]]
+                lows = [up[1] - down[1], down[0] - up[0]]
+                if t == 0:
+                    tops = [jnp.where(first_row, x, y) for x, y in zip(up, tops)]
+                    lows = [jnp.where(first_row, x, y) for x, y in zip(down, lows)]
+                joined = [jnp.concatenate(pair, 0) for pair in zip(tops, lows)]
                 for j in range(4):
                     at = (4 * q + j) * SUB + t * 16
                     shift = (rights[j] + (BLK - SUB * j)) & (BLK - 1)
@@ -528,26 +537,29 @@
     corner = jnp.zeros((1, OWNED * SUB), jnp.int32)
     for s in range(OWNED):
         corner = jnp.where(lax.shift_right_logical(lane, 5) == s, offset[0, s], corner)
-    yy = y_of(lax.shift_right_logical(lane, 4) & 1, lax.shift_right_logical(lane, 3) & 1, lane & 7)
+    high = (lax.shift_right_logical(lane, 4) & 1) * 8 + (lane & 7)
+    low_half = (lane & 8) == 0
+    yy = jnp.where(low_half | (high > 0), 16 + high, 0)
+    use_cos = low_half | (high == 0)
 
     def turned(at, y):
         return sincos_turns(((at * y) & (SUB - 1)).astype(jnp.float32) * (1.0 / SUB))
 
     s_at, c_at = turned(iota((TILE, BLK), 0), jnp.broadcast_to(yy[:, 0:BLK], (TILE, BLK)))
-    s_at, c_at = jnp.concatenate([s_at] * 4, 1), jnp.concatenate([c_at] * 4, 1)
+    use_cos = jnp.broadcast_to(use_cos[:, 0:BLK], (TILE, BLK))
+    first = jnp.concatenate([jnp.where(use_cos, c_at, s_at)] * 4, 1)
+    second = jnp.concatenate([jnp.where(use_cos, s_at, -c_at)] * 4, 1)
     s_corner, c_corner = turned(corner, yy)
-    cy = c_at * c_corner + s_at * s_corner
-    sy = s_at * c_corner - c_at * s_corner
     ky = iota((TILE, OWNED * SUB), 0) - corner
     inside = (ky >= 0) & (ky < SUB)
-    h = jnp.concatenate([jnp.where(inside, cy, 0.0), jnp.where(inside, -sy, 0.0)], 0)
-    h_hi, h_lo = split(h)
-    h_all = jnp.concatenate([h_hi, h_hi, h_lo], 1)
+    h_hi, h_lo = split(jnp.where(inside, first * c_corner + second * s_corner, 0.0))
+    h_both = jnp.concatenate([h_hi, h_lo], 0)
     for p in range(4):
         b_hi, b_lo = split(spread[p])
-        o = dot_nn(h_all, jnp.concatenate([b_hi, b_lo, b_hi], 0))
-        tile[p] = o[0:TILE, 0:BLK] - o[TILE:, BLK:]
-        tile[p + 4] = o[0:TILE, BLK:] + o[TILE:, 0:BLK]
+        o = dot_nn(h_both, b_hi)
+        o = o[0:TILE, :] + o[TILE:, :] + dot_nn(h_hi, b_lo)
+        tile[p] = o[:, 0:BLK]
+        tile[p + 4] = o[:, BLK:]
 
 
 def grid_tile(info, offset, taper, got):

time: 48.9 us -> 49.2 us (level)
  the two profiles are of different devices: /device:TPU:128 before, /device:TPU:1 now
where the time goes in v5:
time: 49.2 us; the launch traced here: 49 us
  Pallas kernels  49 us (100%)
    pallas_call x1, Pallas kernels, exchange(): pl.pallas_call(exchange_kernel, out_shape=(jax.ShapeDtypeStruct((OWNERS *...  23.7 us
    pallas_call x1, Pallas kernels, grid_tile(): pl.pallas_call(grid_kernel, out_shape=jax.ShapeDtypeStruct((8, TILE, TILE...  12.9 us
    pallas_call x1, Pallas kernels, sum_over_freq(): pl.pallas_call(gather_kernel, out_shape=jax.ShapeDtypeStruct((GROUPS, 8,...  10.6 us
    pallas_call x1, Pallas kernels, sum_over_freq(): pl.pallas_call(sum_kernel, out_shape=jax.ShapeDtypeStruct((strip, 8, TILE...  1.73 us

profile of v5, /device:TPU:1, one launch (start us, length us, event | category | flops | bytes accessed | tf_op | source)
XLA Modules:
  0.0 49.0 jit_solution(17038541403748738276)
XLA Ops:
  0.0 23.7 %exchange.1 = (f32[768,128]{1,0:T(8,128)}, s32[8,128]{1,0:T(8,128)}) custom-call(s32[1,32]{1,0:T(1,128)} %bitcast.9, s32[1,32]{1,0:T(1,128)} %slot.1, s32[1,32]{1,0:T(1,128)} %count.1, f32[32,8,128]{2,1,0:T(8,128)} %bitcast.5, f32[32,2,128]{2,1,0:T(2,128)} %bitcast.6, f32[32,128]{1,0:T(8,128)} %bitcast.7), custom_call_target="tpu_custom_call" | custom-call | tf_op jit(solution)/shard_map/exchange/pallas_call | solution.py:176
  23.8 12.9 %grid_tile.1.tile = f32[8,128,128]{2,1,0:T(8,128)} custom-call(s32[8,128]{1,0:T(8,128)} %get-tuple-element.7.info, s32[2,16]{1,0:T(2,128)} %bitcast.8, f32[32,32]{1,0:T(8,128)} %taper.1, f32[768,128]{1,0:T(8,128)} %get-tuple-element.8.got), custom_call_target="tpu_custom_call" | custom-call | tf_op jit(solution)/shard_map/grid_tile/pallas_call | solution.py:575
  36.7 10.6 %gather_over_freq.1.parts = f32[8,8,16,128]{3,2,1,0:T(8,128)} custom-call(f32[8,128,128]{2,1,0:T(8,128)} %grid_tile.1.tile), custom_call_target="tpu_custom_call" | custom-call | tf_op jit(solution)/shard_map/gather_over_freq/pallas_call | solution.py:652
  47.3 1.7 %sum_over_freq.1 = f32[16,8,128]{2,1,0:T(8,128)} custom-call(f32[8,8,16,128]{3,2,1,0:T(8,128)} %gather_over_freq.1.parts), custom_call_target="tpu_custom_call" | custom-call | tf_op jit(solution)/shard_map/sum_over_freq/pallas_call | solution.py:666
